TPU v7x, 128 devices: a whole 4x4x4 slice. The times are simulated.
128 devices in a mesh: cone: 8 (over x_lo, y), con: 16 (over z, x_hi, core).
Axes of the slice: x: 4 (x_hi: 2, x_lo: 2; x = x_hi * 2 + x_lo), y: 4, z: 4, core: 2. Of those that a mesh axis runs over, the one named last changes fastest.
Arguments:
- vectors: bfloat16 [8, 16384, 1024], P('cone', 'con'), may hold values from -0.1875 to 0.1875
- primal: bfloat16 [8, 1024, 1024], P('cone'), may hold values from -8 to 8, as said below
- dual_inverse: bfloat16 [8, 1024, 1024], P('cone'), may hold values from -8 to 8, as said below
- touches: int32 [8, 16], P('cone'), may hold values from 0 to 1, as said below
Outputs:
- slab: float32 [4096, 16384], P('cone', 'con')
Inputs may be any that keep to these rules, and one draw needn't show every extreme that they name: `primal`: symmetric and positive definite in every cone. `dual_inverse`: symmetric and positive definite in every cone. Every constraint block touches at least one cone.
All inputs are finite; a program needn't handle non-finite values.
Results may differ from a plain program's by a relative error of at most 0.00079.
Values may be sent and summed in bfloat16 or wider, within the bound.
A program may use at most 128 MiB of HBM per device.

v0:
```python
import jax
import jax.numpy as jnp
from jax import lax
from jax.sharding import PartitionSpec as P

PANEL = 512


def broadcast(value, axis, source):
    kept = jnp.where(lax.axis_index(axis) == source, value, 0).astype(value.dtype)
    return lax.psum(kept, axis)


def shards(vectors, primal, dual_inverse, touches):
    con_count = lax.axis_size("con")
    cone_count = lax.axis_size("cone")
    con_place = lax.axis_index("con")
    cone_place = lax.axis_index("cone")
    per_block = vectors.shape[1]
    row_dev = PANEL * cone_count // con_count
    owners = con_count // cone_count
    touched = touches[0]
    own_flag = lax.dynamic_index_in_dim(touched, con_place, 0, keepdims=False)
    own_vectors = vectors[0] * own_flag.astype(jnp.bfloat16)
    primal_block = primal[0]
    dual_block = dual_inverse[0]
    leading = own_vectors[:row_dev]
    local_primal = jnp.dot(leading, primal_block, preferred_element_type=jnp.float32).astype(
        jnp.bfloat16
    )
    local_dual = jnp.dot(leading, dual_block, preferred_element_type=jnp.float32).astype(
        jnp.bfloat16
    )
    row_primal, row_dual = (
        lax.all_gather(local_primal, "con", axis=0, tiled=True),
        lax.all_gather(local_dual, "con", axis=0, tiled=True),
    )
    contract = (((1,), (1,)), ((), ()))
    gram_primal = lax.dot_general(
        row_primal, own_vectors, contract, preferred_element_type=jnp.float32
    )
    gram_dual = lax.dot_general(row_dual, own_vectors, contract, preferred_element_type=jnp.float32)
    schur_slab = lax.psum_scatter(gram_primal * gram_dual, "cone", scatter_dimension=0, tiled=True)
    panel_block = broadcast(schur_slab, "cone", 0)
    leading_columns = panel_block[:, :row_dev]
    gathered = lax.all_gather(leading_columns, "con", axis=1, tiled=True)
    pivot_source = gathered[:, :PANEL]
    block_source = lax.dynamic_slice_in_dim(gathered, cone_place * PANEL, PANEL, 1)
    pivot_matrix = (pivot_source + pivot_source.T) * 0.5
    lower_factor = jnp.linalg.cholesky(pivot_matrix)
    combined = jnp.concatenate([panel_block, block_source], axis=1)
    solved = jax.scipy.linalg.solve_triangular(lower_factor, combined, lower=True)
    factor_rows = solved[:, :per_block]
    row_factor = solved[:, per_block:]
    updated = schur_slab - jnp.einsum(
        "kr,kc->rc", row_factor, factor_rows, precision=lax.Precision.HIGHEST
    )
    local_columns = jnp.arange(per_block, dtype=jnp.int32)
    pivot_column = (con_place < owners) & (local_columns < row_dev)
    remaining = jnp.where(pivot_column[None, :], 0.0, updated)
    return jnp.where(cone_place == 0, factor_rows, remaining)


def solution(mesh):
    in_specs = (
        P("cone", "con", None),
        P("cone", None, None),
        P("cone", None, None),
        P("cone", None),
    )
    out_specs = P("cone", "con")
    return jax.shard_map(shards, mesh=mesh, in_specs=in_specs, out_specs=out_specs, check_vma=False)
```

profile of v0, /device:TPU:25, one launch (start us, length us, event | category | flops | bytes accessed | tf_op | source)
XLA Modules:
  0.0 704.1 jit_solution(17182167605988030859)
XLA Ops:
  13.2 3.4 fusion.22
  16.7 72.3 %all-gather.4.cloned.1.call-done = bf16[4096,1024]{1,0:T(8,128)(2,1)} async-done(((bf16[256,1024]{1,0:T(8,128)(2,1)}), bf16[4096,1024]{1,0:T(8,128)(2,1)}) %all-gather.4.cloned.1.call-update) | async-done | bytes 8388624 | tf_op jit(solution)/shard_map/all_gather | solution.py:35
  89.0 14.4 %fusion.8 = f32[4096,1024]{0,1:T(8,128)} fusion(bf16[4096,1024]{1,0:T(8,128)(2,1)} %all-gather.4.cloned.1.call-done, bf16[1,1024,1024]{2,1,0:T(8,128)(2,1)S(1)} %copy-done.10), kind=kOutput, calls=%fused_computation.21 | convolution fusion | flops 8589934592 | bytes 27262976 | tf_op jit(solution)/shard_map/dot_general | solution.py:39
  103.4 58.9 %all-gather.6.cloned.1.call-done = bf16[4096,1024]{1,0:T(8,128)(2,1)} async-done(((bf16[256,1024]{1,0:T(8,128)(2,1)}), bf16[4096,1024]{1,0:T(8,128)(2,1)}) %all-gather.6.cloned.1.call-update) | async-done | bytes 8388624 | tf_op jit(solution)/shard_map/all_gather | solution.py:36
  162.3 19.5 %convolution_multiply_fusion = f32[4096,1024]{0,1:T(8,128)} fusion(f32[4096,1024]{0,1:T(8,128)} %fusion.8, bf16[4096,1024]{1,0:T(8,128)(2,1)} %all-gather.6.cloned.1.call-done, bf16[1,1024,1024]{2,1,0:T(8,128)(2,1)S(1)} %copy-done.10), kind=kOutput, calls=%fused_computation.2 | convolution fusion | flops 8594128896 | bytes 44040192 | tf_op jit(solution)/shard_map/dot_general | solution.py:42
  181.9 166.5 %reduce-scatter.2.cloned.1.call-done = f32[512,1024]{0,1:T(8,128)} async-done(((f32[4096,1024]{0,1:T(8,128)}), f32[512,1024]{0,1:T(8,128)}) %reduce-scatter.2.cloned.1.call-update) | async-done | bytes 2097168 | tf_op jit(solution)/shard_map/reduce_scatter | solution.py:43
  350.2 79.7 %all-reduce.3.cloned.1.call-done = f32[512,1024]{0,1:T(8,128)} async-done(((f32[512,1024]{0,1:T(8,128)}), f32[512,1024]{0,1:T(8,128)}) %all-reduce.3.cloned.1.call-update) | async-done | bytes 2097168 | tf_op jit(solution)/shard_map/psum | solution.py:11
  431.8 78.7 %all-gather.8.cloned.1.call-done = f32[512,4096]{0,1:T(8,128)} async-done(((f32[512,256]{0,1:T(8,128)}), f32[512,4096]{0,1:T(8,128)}) %all-gather.8.cloned.1.call-update) | async-done | bytes 8388624 | tf_op jit(solution)/shard_map/all_gather | solution.py:46
  515.6 11.7 %cholesky.104 = f32[128,128]{1,0:T(8,128)S(1)} custom-call(f32[128,128]{1,0:T(8,128)S(1)} %cholesky.266), custom_call_target="Cholesky" | custom-call | tf_op jit(solution)/shard_map/jit(cholesky)/cholesky | solution.py:50
  527.5 9.8 %custom-call.31 = f32[1,128,128]{1,2,0:T(8,128)S(1)} custom-call(f32[1,128,128]{2,1,0:T(8,128)S(1)} %get-tuple-element.34), custom_call_target="InvertDiagBlocksLowerTriangular" | custom-call | tf_op jit(solution)/shard_map/jit(cholesky)/cholesky | solution.py:50
  539.8 11.7 %cholesky.217 = f32[128,128]{1,0:T(8,128)S(1)} custom-call(f32[128,128]{1,0:T(8,128)S(1)} %cholesky.270), custom_call_target="Cholesky" | custom-call | tf_op jit(solution)/shard_map/jit(cholesky)/cholesky | solution.py:50
  551.5 10.2 %custom-call.32 = f32[1,128,128]{1,2,0:T(8,128)S(1)} custom-call(f32[1,128,128]{2,1,0:T(8,128)S(1)} %get-tuple-element.31), custom_call_target="InvertDiagBlocksLowerTriangular" | custom-call | tf_op jit(solution)/shard_map/jit(cholesky)/cholesky | solution.py:50
  564.3 11.7 %cholesky.238 = f32[128,128]{1,0:T(8,128)S(1)} custom-call(f32[128,128]{1,0:T(8,128)S(1)} %cholesky.275), custom_call_target="Cholesky" | custom-call | tf_op jit(solution)/shard_map/jit(cholesky)/cholesky | solution.py:50
  577.3 9.8 %custom-call.33 = f32[1,128,128]{1,2,0:T(8,128)S(1)} custom-call(f32[1,128,128]{2,1,0:T(8,128)S(1)} %get-tuple-element.28), custom_call_target="InvertDiagBlocksLowerTriangular" | custom-call | tf_op jit(solution)/shard_map/jit(cholesky)/cholesky | solution.py:50
  589.4 11.9 %cholesky.255 = f32[128,128]{1,0:T(8,128)S(1)} custom-call(f32[128,128]{1,0:T(8,128)S(1)} %convolution_subtract_fusion.5), custom_call_target="Cholesky" | custom-call | tf_op jit(solution)/shard_map/jit(cholesky)/cholesky | solution.py:50
  608.0 13.5 %while.1 = (s32[]{:T(128)}, f32[512,512]{1,0:T(8,128)}, s32[4,2]{0,1:T(2,128)S(1)}, f32[4,128,128]{2,1,0:T(8,128)}, s32[]{:T(128)}) while((s32[]{:T(128)}, f32[512,512]{1,0:T(8,128)}, s32[4,2]{0,1:T(2,128)S(1)}, f32[4,128,128]{2,1,0:T(8,128)}, s32[]{:T(128)}) %tuple.28), condition=%wide.while_cond, body=%wide.while_body.sunk | while | flops 2 | bytes 132705 | solution.py:52
  608.6 2.8 bitcast_dynamic-update-slice_fusion.2
  612.0 2.8 bitcast_dynamic-update-slice_fusion.2
  615.4 2.8 bitcast_dynamic-update-slice_fusion.2
  621.6 40.1 %custom-call.34 = f32[4,128,128]{1,2,0:T(8,128)S(1)} custom-call(f32[4,128,128]{2,1,0:T(8,128)} %get-tuple-element.12), custom_call_target="InvertDiagBlocksLowerTriangular" | custom-call | tf_op jit(solution)/shard_map/jit(_solve_triangular)/triangular_solve | solution.py:52
  672.4 4.1 convolution_subtract_fusion
  680.5 6.0 convolution_subtract_fusion.1
  689.5 5.0 select_select_fusion
  694.5 2.9 copy.14
  (82 shorter events, 51.3 us)
Async XLA Ops:
  6.5 5.1 copy-start
  6.5 82.4 %all-gather.4.cloned.1.call-start = ((), (), s32[]{:S(2)}) async-start(), calls=%async_computation.1 | async-start | bytes 8912896 | tf_op jit(solution)/shard_map/all_gather | solution.py:35
  10.3 1.3 copy-start.9
  13.2 75.8 %copy-start.10 = (bf16[1,1024,1024]{2,1,0:T(8,128)(2,1)S(1)}, bf16[1,1024,1024]{2,1,0:T(8,128)(2,1)}, u32[]{:S(2)}) copy-start(bf16[1,1024,1024]{2,1,0:T(8,128)(2,1)} %copy-done.9) | copy-start | bytes 6291460
  13.2 149.2 %all-gather.6.cloned.1.call-start = ((), (), s32[]{:S(2)}) async-start(), calls=%async_computation.2 | async-start | bytes 8912896 | tf_op jit(solution)/shard_map/all_gather | solution.py:36
  16.6 331.8 %reduce-scatter.2.cloned.1.call-start = ((), (), s32[]{:S(2)}) async-start(), calls=%async_computation.3 | async-start | bytes 18874368 | tf_op jit(solution)/shard_map/reduce_scatter | solution.py:43
  181.9 248.0 %all-reduce.3.cloned.1.call-start = ((), (), s32[]{:S(2)}) async-start(), calls=%async_computation.4 | async-start | bytes 4194304 | tf_op jit(solution)/shard_map/psum | solution.py:11
  350.0 160.5 %all-gather.8.cloned.1.call-start = ((), (), s32[]{:S(2)}) async-start(), calls=%async_computation.5 | async-start | bytes 8912896 | tf_op jit(solution)/shard_map/all_gather | solution.py:46
  514.6 1.0 copy-start.8
  562.0 1.0 copy-start.7
  564.3 97.4 %copy-start.2 = (f32[512,1024]{0,1:T(8,128)S(1)}, f32[512,1024]{0,1:T(8,128)}, u32[]{:S(2)}) copy-start(f32[512,1024]{0,1:T(8,128)} %all-reduce.3.cloned.1.call-done) | copy-start | bytes 6291460
  680.5 6.8 copy-start.6
  686.5 1.1 copy-start.4
  686.5 1.4 copy-start.5
  687.9 1.6 copy-start.3
  689.5 7.9 %copy-start.1 = (bf16[1,1024,1024]{2,1,0:T(8,128)(2,1)S(1)}, bf16[1,1024,1024]{2,1,0:T(8,128)(2,1)}, u32[]{:S(2)}) copy-start(bf16[1,1024,1024]{2,1,0:T(8,128)(2,1)} %param.5) | copy-start | bytes 6291460
Sparse Core Ops, SparseCore 0:
  13.3 75.6 all-gather.3
  91.4 70.8 all-gather.5
  182.0 166.3 reduce-scatter.1
  350.8 79.0 all-reduce.2
  432.2 78.2 all-gather.7
where the time goes:
time: 712 us; the launch traced here: 704 us
  waiting for transfers between devices  456 us (64%)
  other arithmetic  130 us (18%)
  matrix products  68.9 us (10%)
  local copies, waits for them, and re-layouts  32.9 us (5%)
  between operations  16.1 us (2%)
    reduce_scatter x1, waiting for transfers between devices, shards(): lax.psum_scatter(gram_primal * gram_dual, 'cone', scatter_dimension=0, ti...  166 us
    another operation x14, other arithmetic, shards(): lower_factor = jnp.linalg.cholesky(pivot_matrix)  80.2 us
    psum x1, waiting for transfers between devices, broadcast(): return lax.psum(kept, axis)  79.7 us
    all_gather x1, waiting for transfers between devices, shards(): gathered = lax.all_gather(leading_columns, 'con', axis=1, tiled=True)  78.7 us
    all_gather x1, waiting for transfers between devices, shards(): lax.all_gather(local_primal, 'con', axis=0, tiled=True)  72.3 us
    all_gather x1, waiting for transfers between devices, shards(): lax.all_gather(local_dual, 'con', axis=0, tiled=True)  58.9 us
    another operation x4, other arithmetic, shards(): jax.scipy.linalg.solve_triangular(lower_factor, combined, lower=True)  42.7 us
    dot_general x1, matrix products, shards(): lax.dot_general(row_dual, own_vectors, contract, preferred_element_type=j...  19.5 us
  transfers between devices with their start and end apart: 5, of which 5 were waited for; matrix products, arithmetic and copies ran while one was open for 3% of the time, Pallas kernels for 0%

commit v1 on v0

--- a/solution.py
+++ b/solution.py
@@ -1,9 +1,78 @@
 import jax
 import jax.numpy as jnp
 from jax import lax
+from jax.experimental import pallas as pl
+from jax.experimental.pallas import tpu as pltpu
 from jax.sharding import PartitionSpec as P
 
 PANEL = 512
+HI = lax.Precision.HIGHEST
+NB = 128
+
+def tdot(a, b, prec=HI):
+    return lax.dot_general(a, b, (((0,), (0,)), ((), ())), precision=prec, preferred_element_type=jnp.float32)
+
+def micro(R, c):
+    d = {}
+    for j in range(8):
+        col = jnp.broadcast_to(R[:, c + j:c + j + 1], (8, 128))
+        for i in range(j, 8):
+            d[i, j] = jnp.broadcast_to(col[i:i + 1, :], (8, 128))
+    rows = []
+    for i in range(8):
+        rows.append([jnp.broadcast_to(R[i:i + 1, h * 128:(h + 1) * 128], (8, 128)) for h in range(2)])
+    for j in range(8):
+        inv = lax.rsqrt(d[j, j])
+        l = {}
+        for i in range(j + 1, 8):
+            l[i] = d[i, j] * inv
+        rows[j] = [x * inv for x in rows[j]]
+        for k in range(j + 1, 8):
+            for i in range(k, 8):
+                d[i, k] = d[i, k] - l[i] * l[k]
+        for i in range(j + 1, 8):
+            rows[i] = [x - l[i] * y for x, y in zip(rows[i], rows[j])]
+    sub = lax.broadcasted_iota(jnp.int32, (8, 128), 0)
+    outs = []
+    for h in range(2):
+        u = rows[0][h]
+        for i in range(1, 8):
+            u = jnp.where(sub == i, rows[i][h], u)
+        outs.append(u)
+    return jnp.concatenate(outs, axis=1)
+
+def diag_factor(W):
+    lane = lax.broadcasted_iota(jnp.int32, (8, 128), 1)
+    for p in range(16):
+        R = W[8 * p:8 * p + 8, :]
+        U = micro(R, 8 * p)
+        W[8 * p:8 * p + 8, :] = U
+        lo = 8 * (p + 1)
+        if p < 15:
+            full = tdot(U[:, :128], U)
+            W[lo:, :] = W[lo:, :] - full[lo:, :]
+
+def kern(a_ref, s_ref, o_ref, X, W):
+    n = s_ref.shape[1]
+    X[:, :512] = (a_ref[...] + a_ref[...].T) * 0.5
+    X[:, 512:] = s_ref[...]
+    eye = (lax.broadcasted_iota(jnp.int32, (128, 128), 0) == lax.broadcasted_iota(jnp.int32, (128, 128), 1)).astype(jnp.float32)
+    for k in range(4):
+        W[:, :128] = X[k * 128:(k + 1) * 128, k * 128:(k + 1) * 128]
+        W[:, 128:] = eye
+        diag_factor(W)
+        inv = W[:, 128:]
+        lo = (k + 1) * 128
+        X[k * 128:lo, lo:] = lax.dot_general(inv, X[k * 128:lo, lo:], (((1,), (0,)), ((), ())), precision=HI, preferred_element_type=jnp.float32)
+        if k < 3:
+            X[lo:, lo:] = X[lo:, lo:] - tdot(X[k * 128:lo, lo:512], X[k * 128:lo, lo:])
+    o_ref[...] = X[:, 512:]
+
+def run(a, s):
+    n = s.shape[1]
+    return pl.pallas_call(kern, out_shape=jax.ShapeDtypeStruct((512, n), jnp.float32),
+        scratch_shapes=[pltpu.VMEM((512, 512 + n), jnp.float32), pltpu.VMEM((128, 256), jnp.float32)],
+        compiler_params=pltpu.CompilerParams(vmem_limit_bytes=48 << 20))(a, s)
 
 
 def broadcast(value, axis, source):
@@ -46,10 +115,8 @@
     gathered = lax.all_gather(leading_columns, "con", axis=1, tiled=True)
     pivot_source = gathered[:, :PANEL]
     block_source = lax.dynamic_slice_in_dim(gathered, cone_place * PANEL, PANEL, 1)
-    pivot_matrix = (pivot_source + pivot_source.T) * 0.5
-    lower_factor = jnp.linalg.cholesky(pivot_matrix)
     combined = jnp.concatenate([panel_block, block_source], axis=1)
-    solved = jax.scipy.linalg.solve_triangular(lower_factor, combined, lower=True)
+    solved = run(pivot_source, combined)
     factor_rows = solved[:, :per_block]
     row_factor = solved[:, per_block:]
     updated = schur_slab - jnp.einsum(

time: 712 us -> 582 us (0.82)
  other arithmetic: 130 us -> 7.29 us
  Pallas kernels: 0 us -> 44.2 us
  local copies, waits for them, and re-layouts: 32.9 us -> 5.43 us
  matrix products: 68.9 us -> 42.6 us
    another operation x18 -> x0, other arithmetic: 123 us -> none  [the longest x14 80.2 us: shards(): lower_factor = jnp.linalg.cholesky(pivot_matrix)]
    pallas_call x0 -> x1, Pallas kernels: none -> 44.2 us  [run(): pl.pallas_call(kern, out_shape=jax.ShapeDtypeStruct((512, n), jnp.float32...]
    another operation x13 -> x0, matrix products: 25 us -> none  [the longest x7 18.7 us: shards(): jax.scipy.linalg.solve_triangular(lower_factor, combined, lower=True)]
    another operation x20 -> x0, local copies, waits for them, and re-layouts: 20.5 us -> none
where the time goes in v1:
time: 582 us; the launch traced here: 573 us
  waiting for transfers between devices  460 us (79%)
  Pallas kernels  44.2 us (8%)
  matrix products  42.6 us (7%)
  between operations  13.4 us (2%)
  other arithmetic  7.29 us (1%)
    reduce_scatter x1, waiting for transfers between devices, shards(): lax.psum_scatter(gram_primal * gram_dual, 'cone', scatter_dimension=0, ti...  166 us
    all_gather x1, waiting for transfers between devices, shards(): gathered = lax.all_gather(leading_columns, 'con', axis=1, tiled=True)  82.7 us
    psum x1, waiting for transfers between devices, broadcast(): return lax.psum(kept, axis)  79.5 us
    all_gather x1, waiting for transfers between devices, shards(): lax.all_gather(local_primal, 'con', axis=0, tiled=True)  72.3 us
    all_gather x1, waiting for transfers between devices, shards(): lax.all_gather(local_dual, 'con', axis=0, tiled=True)  58.8 us
    pallas_call x1, Pallas kernels, run(): pl.pallas_call(kern, out_shape=jax.ShapeDtypeStruct((512, n), jnp.float32...  44.2 us
    dot_general x1, matrix products, shards(): lax.dot_general(row_dual, own_vectors, contract, preferred_element_type=j...  18.2 us
    dot_general x1, matrix products, shards(): lax.dot_general(row_primal, own_vectors, contract, preferred_element_type...  14.6 us
  transfers between devices with their start and end apart: 5, of which 5 were waited for; matrix products, arithmetic and copies ran while one was open for 3% of the time, Pallas kernels for 0%

profile of v1, /device:TPU:25, one launch (start us, length us, event | category | flops | bytes accessed | tf_op | source)
XLA Modules:
  0.0 573.4 jit_solution(8406717533624341749)
XLA Ops:
  6.5 1.4 fusion.19
  7.9 2.4 broadcast_multiply_fusion
  10.3 1.3 copy-done.4
  11.6 1.5 fusion.11
  13.1 0.0 all-gather.4.cloned.1.call-update
  13.2 0.0 all-gather.6.cloned.1.call-start
  13.2 3.4 fusion.14
  16.6 0.0 reduce-scatter.2.cloned.1.call-start
  16.7 72.3 %all-gather.4.cloned.1.call-done = bf16[4096,1024]{1,0:T(8,128)(2,1)} async-done(((bf16[256,1024]{1,0:T(8,128)(2,1)}), bf16[4096,1024]{1,0:T(8,128)(2,1)}) %all-gather.4.cloned.1.call-update) | async-done | bytes 8388624 | tf_op jit(solution)/shard_map/all_gather | solution.py:104
  89.0 14.6 %fusion.3 = f32[4096,1024]{1,0:T(8,128)} fusion(bf16[4096,1024]{1,0:T(8,128)(2,1)} %all-gather.4.cloned.1.call-done, bf16[1,1024,1024]{2,1,0:T(8,128)(2,1)S(1)} %copy-done.5), kind=kOutput, calls=%fused_computation.5 | convolution fusion | flops 8589934592 | bytes 27262976 | tf_op jit(solution)/shard_map/dot_general | solution.py:108
  103.6 58.8 %all-gather.6.cloned.1.call-done = bf16[4096,1024]{1,0:T(8,128)(2,1)} async-done(((bf16[256,1024]{1,0:T(8,128)(2,1)}), bf16[4096,1024]{1,0:T(8,128)(2,1)}) %all-gather.6.cloned.1.call-update) | async-done | bytes 8388624 | tf_op jit(solution)/shard_map/all_gather | solution.py:105
  162.3 18.2 %convolution_multiply_fusion = f32[4096,1024]{1,0:T(8,128)} fusion(f32[4096,1024]{1,0:T(8,128)} %fusion.3, bf16[4096,1024]{1,0:T(8,128)(2,1)} %all-gather.6.cloned.1.call-done, bf16[1,1024,1024]{2,1,0:T(8,128)(2,1)S(1)} %copy-done.5), kind=kOutput, calls=%fused_computation | convolution fusion | flops 8594128896 | bytes 44040192 | tf_op jit(solution)/shard_map/dot_general | solution.py:111
  180.6 0.0 all-reduce.2.cloned.1.call-start
  180.6 166.5 %reduce-scatter.2.cloned.1.call-done = f32[512,1024]{1,0:T(8,128)} async-done(((f32[4096,1024]{1,0:T(8,128)}), f32[512,1024]{1,0:T(8,128)}) %reduce-scatter.2.cloned.1.call-update) | async-done | bytes 2097168 | tf_op jit(solution)/shard_map/reduce_scatter | solution.py:112
  347.1 1.6 broadcast_select_fusion
  348.8 0.5 all-gather.8.cloned.1.call-start
  349.3 79.5 %all-reduce.2.cloned.1.call-done = f32[512,1024]{1,0:T(8,128)} async-done(((f32[512,1024]{1,0:T(8,128)}), f32[512,1024]{1,0:T(8,128)}) %all-reduce.2.cloned.1.call-update) | async-done | bytes 2097168 | tf_op jit(solution)/shard_map/psum | solution.py:80
  428.8 1.9 slice.25
  430.7 82.7 %all-gather.8.cloned.1.call-done = f32[512,4096]{1,0:T(8,128)} async-done(((f32[512,256]{1,0:T(8,128)}), f32[512,4096]{1,0:T(8,128)}) %all-gather.8.cloned.1.call-update) | async-done | bytes 8388624 | tf_op jit(solution)/shard_map/all_gather | solution.py:115
  513.4 1.9 constant_dynamic-slice_fusion
  515.3 0.4 copy-done.3
  515.6 1.9 pad_maximum_fusion.s_ref
  517.5 44.2 %shard_map.46 = f32[512,1536]{1,0:T(8,128)S(1)} custom-call(f32[512,512]{1,0:T(8,128)S(1)} %get-tuple-element.6.a_ref, f32[512,1536]{1,0:T(8,128)} %pad_maximum_fusion.s_ref), custom_call_target="tpu_custom_call" | custom-call | tf_op jit(solution)/shard_map/pallas_call | solution.py:73
  561.8 4.9 select_select_fusion
  (16 shorter events, 0.1 us)
Async XLA Ops:
  6.5 5.1 copy-start
  6.5 82.5 %all-gather.4.cloned.1.call-start = ((), (), s32[]{:S(2)}) async-start(), calls=%async_computation.1 | async-start | bytes 8912896 | tf_op jit(solution)/shard_map/all_gather | solution.py:104
  10.3 1.3 copy-start.4
  13.2 75.8 %copy-start.5 = (bf16[1,1024,1024]{2,1,0:T(8,128)(2,1)S(1)}, bf16[1,1024,1024]{2,1,0:T(8,128)(2,1)}, u32[]{:S(2)}) copy-start(bf16[1,1024,1024]{2,1,0:T(8,128)(2,1)} %copy-done.4) | copy-start | bytes 6291460
  13.2 149.2 %all-gather.6.cloned.1.call-start = ((), (), s32[]{:S(2)}) async-start(), calls=%async_computation.2 | async-start | bytes 8912896 | tf_op jit(solution)/shard_map/all_gather | solution.py:105
  16.6 330.5 %reduce-scatter.2.cloned.1.call-start = ((), (), s32[]{:S(2)}) async-start(), calls=%async_computation.3 | async-start | bytes 18874368 | tf_op jit(solution)/shard_map/reduce_scatter | solution.py:112
  180.6 248.2 %all-reduce.2.cloned.1.call-start = ((), (), s32[]{:S(2)}) async-start(), calls=%async_computation.4 | async-start | bytes 4194304 | tf_op jit(solution)/shard_map/psum | solution.py:80
  348.8 164.6 %all-gather.8.cloned.1.call-start = ((), (), s32[]{:S(2)}) async-start(), calls=%async_computation.5 | async-start | bytes 8912896 | tf_op jit(solution)/shard_map/all_gather | solution.py:115
  513.4 2.2 copy-start.3
  517.5 44.2 %copy-start.2 = (f32[512,1024]{1,0:T(8,128)S(1)}, f32[512,1024]{1,0:T(8,128)}, u32[]{:S(2)}) copy-start(f32[512,1024]{1,0:T(8,128)} %reduce-scatter.2.cloned.1.call-done) | copy-start | bytes 6291460
  517.5 49.1 %copy-start.1 = (bf16[1,1024,1024]{2,1,0:T(8,128)(2,1)S(1)}, bf16[1,1024,1024]{2,1,0:T(8,128)(2,1)}, u32[]{:S(2)}) copy-start(bf16[1,1024,1024]{2,1,0:T(8,128)(2,1)} %param.5) | copy-start | bytes 6291460
Sparse Core Ops, SparseCore 0:
  13.3 75.6 all-gather.3
  91.5 70.8 all-gather.5
  180.7 166.3 reduce-scatter.1
  349.5 79.2 all-reduce.1
  431.0 82.3 all-gather.7

commit v2 on v0

v2 whole, which is shorter than its diff:
```python
import jax
import jax.numpy as jnp
from jax import lax
from jax.experimental import pallas as pl
from jax.experimental.pallas import tpu as pltpu
from jax.sharding import PartitionSpec as P

PANEL = 512
LEAD = 256
HI = lax.Precision.HIGHEST
F32 = jnp.float32
BF16 = jnp.bfloat16
MESH = pl.DeviceIdType.MESH
STOPS = (3, 6, 9)


def tdot(a, b):
    return lax.dot_general(
        a, b, (((0,), (0,)), ((), ())), precision=HI, preferred_element_type=F32
    )


def hdot(a, b):
    return lax.dot_general(
        a, b, (((1,), (0,)), ((), ())), precision=HI, preferred_element_type=F32
    )


def micro(block, first):
    d = {}
    for j in range(8):
        column = jnp.broadcast_to(block[:, first + j : first + j + 1], (8, 128))
        for i in range(j, 8):
            d[i, j] = jnp.broadcast_to(column[i : i + 1, :], (8, 128))
    rows = [
        [jnp.broadcast_to(block[i : i + 1, h * 128 : (h + 1) * 128], (8, 128)) for h in range(2)]
        for i in range(8)
    ]
    for j in range(8):
        inverse = lax.rsqrt(d[j, j])
        low = {i: d[i, j] * inverse for i in range(j + 1, 8)}
        rows[j] = [x * inverse for x in rows[j]]
        for k in range(j + 1, 8):
            for i in range(k, 8):
                d[i, k] = d[i, k] - low[i] * low[k]
        for i in range(j + 1, 8):
            rows[i] = [x - low[i] * y for x, y in zip(rows[i], rows[j])]
    place = lax.broadcasted_iota(jnp.int32, (8, 128), 0)
    halves = []
    for h in range(2):
        upper = rows[0][h]
        for i in range(1, 8):
            upper = jnp.where(place == i, rows[i][h], upper)
        halves.append(upper)
    return jnp.concatenate(halves, axis=1)


def diagonal_factor(work):
    for p in range(16):
        upper = micro(work[8 * p : 8 * p + 8, :], 8 * p)
        work[8 * p : 8 * p + 8, :] = upper
        low = 8 * (p + 1)
        if p < 15:
            change = tdot(upper[:, :128], upper)
            work[low:, :] = work[low:, :] - change[low:, :]


def solve(X, work):
    square = (128, 128)
    eye = lax.broadcasted_iota(jnp.int32, square, 0) == lax.broadcasted_iota(jnp.int32, square, 1)

    @pl.loop(0, 4)
    def _(k):
        here = pl.ds(pl.multiple_of(k * 128, 128), 128)
        work[:, :128] = X[here, here]
        work[:, 128:] = eye.astype(F32)
        diagonal_factor(work)
        X[here, :] = hdot(work[:, 128:], X[here, :])

        @pl.loop(k + 1, 4)
        def _(r):
            there = pl.ds(pl.multiple_of(r * 128, 128), 128)
            X[there, :] = X[there, :] - tdot(X[here, there], X[here, :])


def encode(h, chunk):
    rows, columns = h.shape
    cut = h.reshape(rows // chunk, chunk, columns)
    peak = jnp.max(jnp.abs(cut), axis=1)
    inverse = jnp.where(peak > 1e-33, 32767.0 / jnp.maximum(peak, 1e-33), 0.0)
    coded = jnp.round(cut * inverse[:, None, :]).astype(jnp.int16)
    return coded.reshape(rows, columns), peak * (1.0 / 32767.0)


def decode(coded, scale, chunk):
    rows, columns = coded.shape
    cut = coded.astype(F32).reshape(rows // chunk, chunk, columns)
    return (cut * scale[:, None, :]).reshape(rows, columns)


def kernel(
    t_ref, v_hbm, p_hbm, d_hbm, out_ref,
    rows, V, Pm, Dm, rp, rd, sendq, recvq, ssc, rsc, acc, panel, psc, pqr, pscr, spread, X, work,
    load_sem, g_recv, g_x, g_z, g_s, pr_send, prs_send, pr_recv, prs_recv, ag_send, ag_recv,
    bq_send, bs_send, bq_recv, bs_recv, c_recv, c_x, c_z, c_s,
):
    c = lax.axis_index("cone")
    b = lax.axis_index("con")
    z = b // 4
    xh = (b // 2) % 2
    core = b % 2
    x_peer = b + 2 - 4 * xh
    sibling = b + 1 - 2 * core
    z_peers = [lax.rem(b + 4 * k, 16) for k in (1, 2, 3)]

    lead = pltpu.make_async_copy(
        v_hbm.at[0, pl.ds(0, LEAD), :], rows.at[pl.ds(LEAD * b, LEAD), :], load_sem.at[0]
    )
    loads = [
        pltpu.make_async_copy(h.at[0], m, load_sem.at[k + 1])
        for k, (h, m) in enumerate(((p_hbm, Pm), (d_hbm, Dm), (v_hbm, V)))
    ]
    lead.start()
    for load in loads:
        load.start()

    barrier = pltpu.get_barrier_semaphore()
    for peer in [x_peer, sibling] + z_peers:
        pl.semaphore_signal(barrier, inc=1, device_id={"con": peer}, device_id_type=MESH)
    for s in range(1, 8):
        pl.semaphore_signal(
            barrier, inc=1, device_id={"cone": lax.rem(c + s, 8)}, device_id_type=MESH
        )
    pl.semaphore_wait(barrier, 12)

    def block_copy(slot, sem, peer):
        ref = rows.at[pl.ds(pl.multiple_of(LEAD * slot, LEAD), LEAD), :]
        return pltpu.make_async_remote_copy(
            src_ref=ref, dst_ref=ref, send_sem=sem, recv_sem=g_recv.at[slot],
            device_id={"con": peer}, device_id_type=MESH,
        )

    def to_sibling(slot):
        return block_copy(slot, g_s.at[slot // 2], sibling)

    def to_z(slot, which):
        return [block_copy(slot, g_z.at[which, k], z_peers[k]) for k in range(3)]

    lead.wait()
    to_x = block_copy(b, g_x, x_peer)
    to_x.start()
    for copy in to_z(b, 0):
        copy.start()
    to_sibling(b).start()

    block_copy(x_peer, g_x, x_peer).wait_recv()
    for copy in to_z(x_peer, 1):
        copy.start()
    to_sibling(x_peer).start()

    def arrive(a):
        @pl.when(a // 2 != z)
        def _():
            slot = 2 * a + core
            block_copy(slot, g_x, x_peer).wait_recv()
            to_sibling(slot).start()

    def arrive_sibling(a):
        block_copy(2 * a + 1 - core, g_x, x_peer).wait_recv()

    own_flag = t_ref[0, b].astype(F32)

    def grams(a, sink):
        here = pl.ds(pl.multiple_of(a * PANEL, PANEL), PANEL)
        first = t_ref[0, 2 * a].astype(F32) * own_flag
        second = t_ref[0, 2 * a + 1].astype(F32) * own_flag
        place = lax.broadcasted_iota(jnp.int32, (PANEL, 256), 0)
        flags = jnp.where(place < LEAD, first, second)

        @pl.loop(0, 4)
        def _(n):
            cs = pl.ds(pl.multiple_of(n * 256, 256), 256)
            rp[:, cs] = jnp.dot(rows[here, :], Pm[:, cs], preferred_element_type=F32).astype(BF16)
            rd[:, cs] = jnp.dot(rows[here, :], Dm[:, cs], preferred_element_type=F32).astype(BF16)

        contract = (((1,), (1,)), ((), ()))

        @pl.loop(0, 4)
        def _(n):
            cs = pl.ds(pl.multiple_of(n * 256, 256), 256)
            gp = lax.dot_general(rp[...], V[cs, :], contract, preferred_element_type=F32)
            gd = lax.dot_general(rd[...], V[cs, :], contract, preferred_element_type=F32)
            sink(cs, gp * gd * flags)

    def panel_sink(cs, h):
        acc[:, cs] = h
        coded, scale = encode(h, 8)
        sendq[0, :, cs] = coded
        psc[:, cs] = scale

    def piece(i, size):
        return pl.ds(pl.multiple_of(i * size, size), size)

    def panel_copy(s, slot):
        peer = lax.rem(c + s, 8)
        return (
            pltpu.make_async_remote_copy(
                src_ref=sendq.at[0, piece(peer, 64), :], dst_ref=pqr.at[slot],
                send_sem=pr_send.at[s], recv_sem=pr_recv.at[slot],
                device_id={"cone": peer}, device_id_type=MESH,
            ),
            pltpu.make_async_remote_copy(
                src_ref=psc.at[piece(peer, 8), :], dst_ref=pscr.at[slot],
                send_sem=prs_send.at[s], recv_sem=prs_recv.at[slot],
                device_id={"cone": peer}, device_id_type=MESH,
            ),
        )

    def sum_copy(s, slot):
        ref = panel.at[piece(slot, 64), :]
        return pltpu.make_async_remote_copy(
            src_ref=ref, dst_ref=ref, send_sem=ag_send.at[s], recv_sem=ag_recv.at[slot],
            device_id={"cone": lax.rem(c + s, 8)}, device_id_type=MESH,
        )

    def bulk_copy(a, slot):
        return (
            pltpu.make_async_remote_copy(
                src_ref=sendq.at[a], dst_ref=recvq.at[slot],
                send_sem=bq_send.at[a], recv_sem=bq_recv.at[slot],
                device_id={"cone": a}, device_id_type=MESH,
            ),
            pltpu.make_async_remote_copy(
                src_ref=ssc.at[a], dst_ref=rsc.at[slot],
                send_sem=bs_send.at[a], recv_sem=bs_recv.at[slot],
                device_id={"cone": a}, device_id_type=MESH,
            ),
        )

    def bulk_step(t):
        a = lax.rem(c + t, 8)
        follow = lax.rem(c + t + 1, 8)

        @pl.when((t < 8) & (follow != 0))
        def _():
            arrive(follow)

        @pl.when(a != 0)
        def _():
            arrive_sibling(a)

            def sink(cs, h):
                @pl.when(a == c)
                def _():
                    acc[:, cs] = h

                @pl.when(a != c)
                def _():
                    coded, scale = encode(h, 32)
                    sendq[a, :, cs] = coded
                    ssc[a, :, cs] = scale

            grams(a, sink)

            @pl.when(a != c)
            def _():
                for copy in bulk_copy(a, c):
                    copy.start()

    def bulk(low, high):
        @pl.loop(low, high)
        def _(t):
            bulk_step(t)

    def spread_copy(kind, slot, sem, peer):
        ref = spread.at[kind, slot]
        return pltpu.make_async_remote_copy(
            src_ref=ref, dst_ref=ref, send_sem=sem, recv_sem=c_recv.at[kind, slot],
            device_id={"con": peer}, device_id_type=MESH,
        )

    homes = [(0, 0), (c // 2, lax.rem(c, 2))]

    def spread_on(kind):
        for k in range(3):
            spread_copy(kind, core, c_z.at[kind, k], z_peers[k]).start()
        spread_copy(kind, core, c_s.at[kind], sibling).start()

    def spread_start(kind):
        z0, x0 = homes[kind]

        @pl.when((z == z0) & (xh == x0))
        def _():
            spread[kind, core] = panel[:, :LEAD]
            spread_copy(kind, core, c_x.at[kind], x_peer).start()
            spread_on(kind)

    def spread_relay(kind):
        z0, x0 = homes[kind]

        @pl.when((z == z0) & (xh != x0))
        def _():
            spread_copy(kind, core, c_x.at[kind], x_peer).wait_recv()
            spread_on(kind)

        @pl.when(z != z0)
        def _():
            spread_copy(kind, core, c_x.at[kind], x_peer).wait_recv()
            spread_copy(kind, core, c_s.at[kind], sibling).start()

    def spread_end(kind):
        z0, x0 = homes[kind]
        spread_copy(kind, core, c_s.at[kind], sibling).wait_send()

        @pl.when(z == z0)
        def _():
            for k in range(3):
                spread_copy(kind, core, c_z.at[kind, k], z_peers[k]).wait_send()

        @pl.when((z == z0) & (xh == x0))
        def _():
            spread_copy(kind, core, c_x.at[kind], x_peer).wait_send()

    arrive(0)
    arrive_sibling(0)
    for load in loads:
        load.wait()
    grams(0, panel_sink)
    for s in range(1, 8):
        for copy in panel_copy(s, c):
            copy.start()

    first = lax.rem(c + 1, 8)

    @pl.when(first != 0)
    def _():
        arrive(first)

    bulk(1, STOPS[0])

    mine = piece(c, 64)
    panel[mine, :] = acc[mine, :]

    @pl.loop(1, 8)
    def _(s):
        source = lax.rem(c + s, 8)
        for copy in panel_copy(s, source):
            copy.wait_recv()
        panel[mine, :] = panel[mine, :] + decode(pqr[source], pscr[source], 8)

    for s in range(1, 8):
        sum_copy(s, c).start()

    bulk(STOPS[0], STOPS[1])

    for s in range(1, 8):
        sum_copy(s, lax.rem(c + s, 8)).wait_recv()
    for kind in range(2):
        spread_start(kind)

    bulk(STOPS[1], STOPS[2])

    for kind in range(2):
        spread_relay(kind)
    for kind in range(2):
        spread_copy(kind, 1 - core, c_s.at[kind], sibling).wait_recv()
    bulk(STOPS[2], 9)

    X[:, :LEAD] = spread[0, 0]
    X[:, LEAD:PANEL] = spread[0, 1]
    pivot = X[:, :PANEL]
    X[:, :PANEL] = (pivot + pivot.T) * 0.5
    X[:, PANEL : PANEL + 1024] = panel[...]
    X[:, PANEL + 1024 : PANEL + 1024 + LEAD] = spread[1, 0]
    X[:, PANEL + 1024 + LEAD :] = spread[1, 1]
    solve(X, work)

    @pl.when(c != 0)
    def _():
        @pl.loop(1, 8)
        def _(s):
            source = lax.rem(c + s, 8)
            for copy in bulk_copy(source, source):
                copy.wait_recv()
            for r in range(4):
                part = pl.ds(r * 128, 128)
                acc[part, :] = acc[part, :] + decode(
                    recvq[source, part, :], rsc[source, pl.ds(r * 4, 4), :], 32
                )

        @pl.loop(0, 4)
        def _(r):
            part = pl.ds(pl.multiple_of(r * 128, 128), 128)
            columns = pl.ds(pl.multiple_of(PANEL + 1024 + r * 128, 128), 128)
            change = tdot(X[:, columns], X[:, PANEL : PANEL + 1024])
            place = lax.broadcasted_iota(jnp.int32, (128, 1024), 1)
            gone = (place < LEAD) & (b < 2)
            out_ref[part, :] = jnp.where(gone, 0.0, acc[part, :] - change)

    @pl.when(c == 0)
    def _():
        out_ref[...] = X[:, PANEL : PANEL + 1024]

    to_x.wait_send()
    for copy in to_z(b, 0) + to_z(x_peer, 1):
        copy.wait_send()

    @pl.loop(0, 8)
    def _(a):
        to_sibling(2 * a + core).wait_send()

    for s in range(1, 8):
        for copy in panel_copy(s, c):
            copy.wait_send()
        sum_copy(s, c).wait_send()

        a = lax.rem(c + s, 8)

        @pl.when(a != 0)
        def _():
            for copy in bulk_copy(a, c):
                copy.wait_send()

    for kind in range(2):
        spread_end(kind)


def shards(vectors, primal, dual_inverse, touches):
    dma = pltpu.SemaphoreType.DMA
    vmem = pltpu.VMEM
    anywhere = pl.BlockSpec(memory_space=pl.ANY)
    return pl.pallas_call(
        kernel,
        out_shape=jax.ShapeDtypeStruct((PANEL, 1024), F32),
        in_specs=[pl.BlockSpec(memory_space=pltpu.SMEM), anywhere, anywhere, anywhere],
        out_specs=pl.BlockSpec(memory_space=pltpu.VMEM),
        scratch_shapes=[
            vmem((4096, 1024), BF16),
            vmem((1024, 1024), BF16),
            vmem((1024, 1024), BF16),
            vmem((1024, 1024), BF16),
            vmem((PANEL, 1024), BF16),
            vmem((PANEL, 1024), BF16),
            vmem((8, PANEL, 1024), jnp.int16),
            vmem((8, PANEL, 1024), jnp.int16),
            vmem((8, 16, 1024), F32),
            vmem((8, 16, 1024), F32),
            vmem((PANEL, 1024), F32),
            vmem((PANEL, 1024), F32),
            vmem((64, 1024), F32),
            vmem((8, 64, 1024), jnp.int16),
            vmem((8, 8, 1024), F32),
            vmem((2, 2, PANEL, LEAD), F32),
            vmem((PANEL, 2048), F32),
            vmem((128, 256), F32),
            dma((4,)), dma((16,)), dma, dma((2, 3)), dma((8,)),
            dma((8,)), dma((8,)), dma((8,)), dma((8,)), dma((8,)), dma((8,)),
            dma((8,)), dma((8,)), dma((8,)), dma((8,)),
            dma((2, 2)), dma((2,)), dma((2, 3)), dma((2,)),
        ],
        compiler_params=pltpu.CompilerParams(
            collective_id=0, has_side_effects=True, vmem_limit_bytes=60 << 20
        ),
    )(touches, vectors, primal, dual_inverse)


def solution(mesh):
    in_specs = (
        P("cone", "con", None),
        P("cone", None, None),
        P("cone", None, None),
        P("cone", None),
    )
    out_specs = P("cone", "con")
    return jax.shard_map(shards, mesh=mesh, in_specs=in_specs, out_specs=out_specs, check_vma=False)
```

time: 712 us -> 321 us (0.45); the launches traced: 704 us -> 321 us
  waiting for transfers between devices: 456 us -> 0 us
  Pallas kernels: 0 us -> 318 us
  other arithmetic: 130 us -> 0 us
  matrix products: 68.9 us -> 0 us
  local copies, waits for them, and re-layouts: 32.9 us -> 3.16 us
  between operations: 16.1 us -> 0.01 us
    pallas_call x0 -> x1, Pallas kernels: none -> 318 us  [shards(): pl.pallas_call(kernel, out_shape=jax.ShapeDtypeStruct((PANEL, 1024), F32)...]
    all_gather x3 -> x0, waiting for transfers between devices: 210 us -> none  [the longest x1 78.7 us: shards(): gathered = lax.all_gather(leading_columns, 'con', axis=1, tiled=True)]
    reduce_scatter x1 -> x0, waiting for transfers between devices: 166 us -> none  [shards(): lax.psum_scatter(gram_primal * gram_dual, 'cone', scatter_dimension=0, ti...]
    another operation x18 -> x0, other arithmetic: 123 us -> none  [the longest x14 80.2 us: shards(): lower_factor = jnp.linalg.cholesky(pivot_matrix)]
    psum x1 -> x0, waiting for transfers between devices: 79.7 us -> none  [broadcast(): return lax.psum(kept, axis)]
    dot_general x5 -> x0, matrix products: 43.9 us -> none  [the longest x1 19.5 us: shards(): lax.dot_general(row_dual, own_vectors, contract, preferred_element_type=j...]
    another operation x13 -> x0, matrix products: 25 us -> none  [the longest x7 18.7 us: shards(): jax.scipy.linalg.solve_triangular(lower_factor, combined, lower=True)]
    another operation x20 -> x0, local copies, waits for them, and re-layouts: 20.5 us -> none
  transfers between devices with their start and end apart: 5 -> 0, of which waited for: 5 -> 0; matrix products, arithmetic and copies ran while one was open for 3% -> 0% of each run, Pallas kernels for 0% -> 0%
where the time goes in v2:
time: 321 us
  Pallas kernels  318 us (99%)
    pallas_call x1, Pallas kernels, shards(): pl.pallas_call(kernel, out_shape=jax.ShapeDtypeStruct((PANEL, 1024), F32)...  318 us

profile of v2, /device:TPU:25, one launch (start us, length us, event | category | flops | bytes accessed | tf_op | source)
XLA Modules:
  0.0 321.1 jit_solution(7495363637307901844)
XLA Ops:
  0.0 317.9 %shard_map.46 = f32[512,1024]{1,0:T(8,128)} custom-call(s32[1,16]{1,0:T(1,128)} %t_ref.1, bf16[1,1024,1024]{2,1,0:T(8,128)(2,1)} %v_hbm.1, bf16[1,1024,1024]{2,1,0:T(8,128)(2,1)} %p_hbm.1, bf16[1,1024,1024]{2,1,0:T(8,128)(2,1)} %d_hbm.1), custom_call_target="tpu_custom_call" | custom-call | tf_op jit(solution)/shard_map/pallas_call | solution.py:432
  317.9 3.2 copy.6

commit v3 on v2

--- a/solution.py
+++ b/solution.py
@@ -11,7 +11,9 @@
 F32 = jnp.float32
 BF16 = jnp.bfloat16
 MESH = pl.DeviceIdType.MESH
-STOPS = (3, 6, 9)
+OFFSETS = ((0, 1), (0, 3), (1, 0), (0, 2), (1, 1), (1, 3), (1, 2), (0, 0))
+FIRST_STEPS = 4
+STEPS_PER_BLOCK = 2
 
 
 def tdot(a, b):
@@ -65,22 +67,34 @@
             work[low:, :] = work[low:, :] - change[low:, :]
 
 
-def solve(X, work):
+def block(i):
+    return pl.ds(pl.multiple_of(i * 128, 128), 128)
+
+
+def factor_step(k, A, inverses, work):
     square = (128, 128)
     eye = lax.broadcasted_iota(jnp.int32, square, 0) == lax.broadcasted_iota(jnp.int32, square, 1)
-
+    here = block(k)
+    work[:, :128] = A[here, here]
+    work[:, 128:] = eye.astype(F32)
+    diagonal_factor(work)
+    inverses[k] = work[:, 128:]
+    A[here, :] = hdot(work[:, 128:], A[here, :])
+
+    @pl.loop(k + 1, 4)
+    def _(r):
+        A[block(r), :] = A[block(r), :] - tdot(A[here, block(r)], A[here, :])
+
+
+def substitute(A, inverses, X):
     @pl.loop(0, 4)
     def _(k):
-        here = pl.ds(pl.multiple_of(k * 128, 128), 128)
-        work[:, :128] = X[here, here]
-        work[:, 128:] = eye.astype(F32)
-        diagonal_factor(work)
-        X[here, :] = hdot(work[:, 128:], X[here, :])
+        here = block(k)
+        X[here, :] = hdot(inverses[k], X[here, :])
 
         @pl.loop(k + 1, 4)
         def _(r):
-            there = pl.ds(pl.multiple_of(r * 128, 128), 128)
-            X[there, :] = X[there, :] - tdot(X[here, there], X[here, :])
+            X[block(r), :] = X[block(r), :] - tdot(A[here, block(r)], X[here, :])
 
 
 def encode(h, chunk):
@@ -100,9 +114,11 @@
 
 def kernel(
     t_ref, v_hbm, p_hbm, d_hbm, out_ref,
-    rows, V, Pm, Dm, rp, rd, sendq, recvq, ssc, rsc, acc, panel, psc, pqr, pscr, spread, X, work,
+    rows, V, Pm, Dm, rp, rd, sendq, recvq, ssc, rsc, acc, psc, pqr, pscr,
+    bpart, brecv, bfull, A, inverses, X, work,
     load_sem, g_recv, g_x, g_z, g_s, pr_send, prs_send, pr_recv, prs_recv, ag_send, ag_recv,
     bq_send, bs_send, bq_recv, bs_recv, c_recv, c_x, c_z, c_s,
+    br_send, br_recv, ba_send, ba_recv, bx_send, bx_recv,
 ):
     c = lax.axis_index("cone")
     b = lax.axis_index("con")
@@ -153,11 +169,6 @@
         copy.start()
     to_sibling(b).start()
 
-    block_copy(x_peer, g_x, x_peer).wait_recv()
-    for copy in to_z(x_peer, 1):
-        copy.start()
-    to_sibling(x_peer).start()
-
     def arrive(a):
         @pl.when(a // 2 != z)
         def _():
@@ -170,12 +181,11 @@
 
     own_flag = t_ref[0, b].astype(F32)
 
-    def grams(a, sink):
+    own_chip = b // 2
+    contract = (((1,), (1,)), ((), ()))
+
+    def products(a):
         here = pl.ds(pl.multiple_of(a * PANEL, PANEL), PANEL)
-        first = t_ref[0, 2 * a].astype(F32) * own_flag
-        second = t_ref[0, 2 * a + 1].astype(F32) * own_flag
-        place = lax.broadcasted_iota(jnp.int32, (PANEL, 256), 0)
-        flags = jnp.where(place < LEAD, first, second)
 
         @pl.loop(0, 4)
         def _(n):
@@ -183,7 +193,11 @@
             rp[:, cs] = jnp.dot(rows[here, :], Pm[:, cs], preferred_element_type=F32).astype(BF16)
             rd[:, cs] = jnp.dot(rows[here, :], Dm[:, cs], preferred_element_type=F32).astype(BF16)
 
-        contract = (((1,), (1,)), ((), ()))
+    def grams(a, sink):
+        first = t_ref[0, 2 * a].astype(F32) * own_flag
+        second = t_ref[0, 2 * a + 1].astype(F32) * own_flag
+        place = lax.broadcasted_iota(jnp.int32, (PANEL, 256), 0)
+        flags = jnp.where(place < LEAD, first, second)
 
         @pl.loop(0, 4)
         def _(n):
@@ -192,14 +206,46 @@
             gd = lax.dot_general(rd[...], V[cs, :], contract, preferred_element_type=F32)
             sink(cs, gp * gd * flags)
 
+    def piece(i, size):
+        return pl.ds(pl.multiple_of(i * size, size), size)
+
+    def pivot_part():
+        half = piece(core, LEAD)
+        row_flag = t_ref[0, core].astype(F32)
+        place = lax.broadcasted_iota(jnp.int32, (LEAD, PANEL), 1)
+        flags = jnp.where(place < LEAD, t_ref[0, 0].astype(F32), t_ref[0, 1].astype(F32)) * row_flag
+        lead_rows = rows[:PANEL, :]
+        gp = lax.dot_general(rp[half, :], lead_rows, contract, preferred_element_type=F32)
+        gd = lax.dot_general(rd[half, :], lead_rows, contract, preferred_element_type=F32)
+        bpart[...] = gp * gd * flags
+
+    def pivot_copy(s, slot):
+        peer = lax.rem(c + s, 8)
+        return pltpu.make_async_remote_copy(
+            src_ref=bpart.at[piece(peer, 32), :], dst_ref=brecv.at[slot],
+            send_sem=br_send.at[s], recv_sem=br_recv.at[slot],
+            device_id={"cone": peer}, device_id_type=MESH,
+        )
+
+    def pivot_sum_copy(s, slot):
+        ref = bfull.at[core, piece(slot, 32), :]
+        return pltpu.make_async_remote_copy(
+            src_ref=ref, dst_ref=ref, send_sem=ba_send.at[s], recv_sem=ba_recv.at[slot],
+            device_id={"cone": lax.rem(c + s, 8)}, device_id_type=MESH,
+        )
+
+    def pivot_half_copy(half):
+        ref = bfull.at[half]
+        return pltpu.make_async_remote_copy(
+            src_ref=ref, dst_ref=ref, send_sem=bx_send, recv_sem=bx_recv,
+            device_id={"con": sibling}, device_id_type=MESH,
+        )
+
     def panel_sink(cs, h):
-        acc[:, cs] = h
+        X[:, cs] = h
         coded, scale = encode(h, 8)
         sendq[0, :, cs] = coded
         psc[:, cs] = scale
-
-    def piece(i, size):
-        return pl.ds(pl.multiple_of(i * size, size), size)
 
     def panel_copy(s, slot):
         peer = lax.rem(c + s, 8)
@@ -217,7 +263,7 @@
         )
 
     def sum_copy(s, slot):
-        ref = panel.at[piece(slot, 64), :]
+        ref = X.at[piece(slot, 64), pl.ds(0, 1024)]
         return pltpu.make_async_remote_copy(
             src_ref=ref, dst_ref=ref, send_sem=ag_send.at[s], recv_sem=ag_recv.at[slot],
             device_id={"cone": lax.rem(c + s, 8)}, device_id_type=MESH,
@@ -237,143 +283,210 @@
             ),
         )
 
-    def bulk_step(t):
-        a = lax.rem(c + t, 8)
-        follow = lax.rem(c + t + 1, 8)
-
-        @pl.when((t < 8) & (follow != 0))
-        def _():
-            arrive(follow)
-
-        @pl.when(a != 0)
-        def _():
-            arrive_sibling(a)
-
-            def sink(cs, h):
-                @pl.when(a == c)
-                def _():
-                    acc[:, cs] = h
-
-                @pl.when(a != c)
-                def _():
-                    coded, scale = encode(h, 32)
-                    sendq[a, :, cs] = coded
-                    ssc[a, :, cs] = scale
-
-            grams(a, sink)
+    def bulk_part(a, part):
+        here = pl.ds(128 * part, 128)
+        return pltpu.make_async_remote_copy(
+            src_ref=sendq.at[a, here, :], dst_ref=recvq.at[c, here, :],
+            send_sem=bq_send.at[a], recv_sem=bq_recv.at[c],
+            device_id={"cone": a}, device_id_type=MESH,
+        )
+
+    def compute(a):
+        def sink(cs, h):
+            @pl.when(a == c)
+            def _():
+                acc[:, cs] = h
 
             @pl.when(a != c)
             def _():
-                for copy in bulk_copy(a, c):
-                    copy.start()
+                coded, scale = encode(h, 32)
+                sendq[a, :, cs] = coded
+                ssc[a, :, cs] = scale
+
+        arrive_sibling(a)
+        products(a)
+        grams(a, sink)
+
+    def target(t):
+        dx = dy = 0
+        for k, (x, y) in enumerate(OFFSETS):
+            dx = jnp.where(t == k + 1, x, dx)
+            dy = jnp.where(t == k + 1, y, dy)
+        return lax.rem(c // 4 + dx, 2) * 4 + lax.rem(lax.rem(c, 4) + dy, 4)
+
+    def issue(low, high):
+        for part in range(4):
+            for t in range(low, high):
+                a = target(t)
+
+                @pl.when(a != 0)
+                def _():
+                    if part == 0:
+                        bulk_copy(a, c)[1].start()
+                    bulk_part(a, part).start()
+
+    def bulk_step(t):
+        a = target(t)
+        follow = target(t + 1)
+
+        @pl.when((t < 8) & (follow != 0))
+        def _():
+            arrive(follow)
+
+        @pl.when((a != 0) & (a != own_chip))
+        def _():
+            compute(a)
+
+        @pl.when((t == 3))
+        def _():
+            issue(1, 4)
+
+        @pl.when((t == 7))
+        def _():
+            issue(4, 8)
 
     def bulk(low, high):
         @pl.loop(low, high)
         def _(t):
             bulk_step(t)
 
-    def spread_copy(kind, slot, sem, peer):
-        ref = spread.at[kind, slot]
-        return pltpu.make_async_remote_copy(
-            src_ref=ref, dst_ref=ref, send_sem=sem, recv_sem=c_recv.at[kind, slot],
+    def spread_copy(slot, sem, peer):
+        ref = X.at[:, pl.ds(pl.multiple_of(1024 + slot * LEAD, LEAD), LEAD)]
+        return pltpu.make_async_remote_copy(
+            src_ref=ref, dst_ref=ref, send_sem=sem, recv_sem=c_recv.at[slot],
             device_id={"con": peer}, device_id_type=MESH,
         )
 
-    homes = [(0, 0), (c // 2, lax.rem(c, 2))]
-
-    def spread_on(kind):
+    at_home_z = z == c // 2
+    at_home_x = xh == lax.rem(c, 2)
+
+    def spread_on():
         for k in range(3):
-            spread_copy(kind, core, c_z.at[kind, k], z_peers[k]).start()
-        spread_copy(kind, core, c_s.at[kind], sibling).start()
-
-    def spread_start(kind):
-        z0, x0 = homes[kind]
-
-        @pl.when((z == z0) & (xh == x0))
-        def _():
-            spread[kind, core] = panel[:, :LEAD]
-            spread_copy(kind, core, c_x.at[kind], x_peer).start()
-            spread_on(kind)
-
-    def spread_relay(kind):
-        z0, x0 = homes[kind]
-
-        @pl.when((z == z0) & (xh != x0))
-        def _():
-            spread_copy(kind, core, c_x.at[kind], x_peer).wait_recv()
-            spread_on(kind)
-
-        @pl.when(z != z0)
-        def _():
-            spread_copy(kind, core, c_x.at[kind], x_peer).wait_recv()
-            spread_copy(kind, core, c_s.at[kind], sibling).start()
-
-    def spread_end(kind):
-        z0, x0 = homes[kind]
-        spread_copy(kind, core, c_s.at[kind], sibling).wait_send()
-
-        @pl.when(z == z0)
+            spread_copy(core, c_z.at[k], z_peers[k]).start()
+        spread_copy(core, c_s, sibling).start()
+
+    def spread_start():
+        @pl.when(at_home_z & at_home_x)
+        def _():
+            X[:, pl.ds(pl.multiple_of(1024 + core * LEAD, LEAD), LEAD)] = X[:, :LEAD]
+            spread_copy(core, c_x, x_peer).start()
+            spread_on()
+
+    def spread_relay():
+        @pl.when(at_home_z & (xh != lax.rem(c, 2)))
+        def _():
+            spread_copy(core, c_x, x_peer).wait_recv()
+            spread_on()
+
+    def spread_relay_far():
+        @pl.when(z != c // 2)
+        def _():
+            spread_copy(core, c_x, x_peer).wait_recv()
+            spread_copy(core, c_s, sibling).start()
+
+    def spread_end():
+        spread_copy(core, c_s, sibling).wait_send()
+
+        @pl.when(at_home_z)
         def _():
             for k in range(3):
-                spread_copy(kind, core, c_z.at[kind, k], z_peers[k]).wait_send()
-
-        @pl.when((z == z0) & (xh == x0))
-        def _():
-            spread_copy(kind, core, c_x.at[kind], x_peer).wait_send()
+                spread_copy(core, c_z.at[k], z_peers[k]).wait_send()
+
+        @pl.when(at_home_z & at_home_x)
+        def _():
+            spread_copy(core, c_x, x_peer).wait_send()
+
+    for load in loads:
+        load.wait()
+
+    @pl.when(own_chip != 0)
+    def _():
+        compute(own_chip)
+
+    block_copy(x_peer, g_x, x_peer).wait_recv()
+    for copy in to_z(x_peer, 1):
+        copy.start()
+    to_sibling(x_peer).start()
 
     arrive(0)
     arrive_sibling(0)
-    for load in loads:
-        load.wait()
+    products(0)
+    pivot_part()
+    for s in range(1, 8):
+        pivot_copy(s, c).start()
+
     grams(0, panel_sink)
+
+    half_piece = piece(c, 32)
+    bfull[core, half_piece, :] = bpart[half_piece, :]
+
+    @pl.loop(1, 8)
+    def _(s):
+        source = lax.rem(c + s, 8)
+        pivot_copy(s, source).wait_recv()
+        bfull[core, half_piece, :] = bfull[core, half_piece, :] + brecv[source]
+
+    for s in range(1, 8):
+        pivot_sum_copy(s, c).start()
     for s in range(1, 8):
         for copy in panel_copy(s, c):
             copy.start()
 
-    first = lax.rem(c + 1, 8)
-
-    @pl.when(first != 0)
+    follow = target(1)
+
+    @pl.when(follow != 0)
     def _():
-        arrive(first)
-
-    bulk(1, STOPS[0])
+        arrive(follow)
+
+    bulk(1, FIRST_STEPS)
+
+    for s in range(1, 8):
+        pivot_sum_copy(s, lax.rem(c + s, 8)).wait_recv()
+    pivot_half_copy(core).start()
 
     mine = piece(c, 64)
-    panel[mine, :] = acc[mine, :]
 
     @pl.loop(1, 8)
     def _(s):
         source = lax.rem(c + s, 8)
         for copy in panel_copy(s, source):
             copy.wait_recv()
-        panel[mine, :] = panel[mine, :] + decode(pqr[source], pscr[source], 8)
+        X[mine, :1024] = X[mine, :1024] + decode(pqr[source], pscr[source], 8)
 
     for s in range(1, 8):
         sum_copy(s, c).start()
 
-    bulk(STOPS[0], STOPS[1])
-
-    for s in range(1, 8):
-        sum_copy(s, lax.rem(c + s, 8)).wait_recv()
-    for kind in range(2):
-        spread_start(kind)
-
-    bulk(STOPS[1], STOPS[2])
-
-    for kind in range(2):
-        spread_relay(kind)
-    for kind in range(2):
-        spread_copy(kind, 1 - core, c_s.at[kind], sibling).wait_recv()
-    bulk(STOPS[2], 9)
-
-    X[:, :LEAD] = spread[0, 0]
-    X[:, LEAD:PANEL] = spread[0, 1]
-    pivot = X[:, :PANEL]
-    X[:, :PANEL] = (pivot + pivot.T) * 0.5
-    X[:, PANEL : PANEL + 1024] = panel[...]
-    X[:, PANEL + 1024 : PANEL + 1024 + LEAD] = spread[1, 0]
-    X[:, PANEL + 1024 + LEAD :] = spread[1, 1]
-    solve(X, work)
+    pivot_half_copy(1 - core).wait_recv()
+    A[:LEAD, :] = bfull[0]
+    A[LEAD:, :] = bfull[1]
+    A[...] = (A[...] + A[...].T) * 0.5
+
+    @pl.loop(0, 4)
+    def _(k):
+        factor_step(k, A, inverses, work)
+
+        @pl.when(k == 1)
+        def _():
+            for s in range(1, 8):
+                sum_copy(s, lax.rem(c + s, 8)).wait_recv()
+            spread_start()
+
+        @pl.when(k == 2)
+        def _():
+            spread_relay()
+
+        @pl.when(k == 3)
+        def _():
+            spread_relay_far()
+
+        low = FIRST_STEPS + STEPS_PER_BLOCK * k
+        bulk(low, jnp.where(k == 3, 9, jnp.minimum(low + STEPS_PER_BLOCK, 9)))
+
+    spread_copy(1 - core, c_s, sibling).wait_recv()
+    spread_end()
+    for s in range(1, 8):
+        sum_copy(s, c).wait_send()
+    substitute(A, inverses, X)
 
     @pl.when(c != 0)
     def _():
@@ -390,16 +503,15 @@
 
         @pl.loop(0, 4)
         def _(r):
-            part = pl.ds(pl.multiple_of(r * 128, 128), 128)
-            columns = pl.ds(pl.multiple_of(PANEL + 1024 + r * 128, 128), 128)
-            change = tdot(X[:, columns], X[:, PANEL : PANEL + 1024])
+            part = block(r)
+            change = tdot(X[:, block(8 + r)], X[:, :1024])
             place = lax.broadcasted_iota(jnp.int32, (128, 1024), 1)
             gone = (place < LEAD) & (b < 2)
             out_ref[part, :] = jnp.where(gone, 0.0, acc[part, :] - change)
 
     @pl.when(c == 0)
     def _():
-        out_ref[...] = X[:, PANEL : PANEL + 1024]
+        out_ref[...] = X[:, :1024]
 
     to_x.wait_send()
     for copy in to_z(b, 0) + to_z(x_peer, 1):
@@ -412,7 +524,6 @@
     for s in range(1, 8):
         for copy in panel_copy(s, c):
             copy.wait_send()
-        sum_copy(s, c).wait_send()
 
         a = lax.rem(c + s, 8)
 
@@ -421,8 +532,10 @@
             for copy in bulk_copy(a, c):
                 copy.wait_send()
 
-    for kind in range(2):
-        spread_end(kind)
+        pivot_copy(s, c).wait_send()
+        pivot_sum_copy(s, c).wait_send()
+
+    pivot_half_copy(core).wait_send()
 
 
 def shards(vectors, primal, dual_inverse, touches):
@@ -446,17 +559,21 @@
             vmem((8, 16, 1024), F32),
             vmem((8, 16, 1024), F32),
             vmem((PANEL, 1024), F32),
-            vmem((PANEL, 1024), F32),
             vmem((64, 1024), F32),
             vmem((8, 64, 1024), jnp.int16),
             vmem((8, 8, 1024), F32),
-            vmem((2, 2, PANEL, LEAD), F32),
-            vmem((PANEL, 2048), F32),
+            vmem((LEAD, PANEL), F32),
+            vmem((8, 32, PANEL), F32),
+            vmem((2, LEAD, PANEL), F32),
+            vmem((PANEL, PANEL), F32),
+            vmem((4, 128, 128), F32),
+            vmem((PANEL, 1536), F32),
             vmem((128, 256), F32),
             dma((4,)), dma((16,)), dma, dma((2, 3)), dma((8,)),
             dma((8,)), dma((8,)), dma((8,)), dma((8,)), dma((8,)), dma((8,)),
             dma((8,)), dma((8,)), dma((8,)), dma((8,)),
-            dma((2, 2)), dma((2,)), dma((2, 3)), dma((2,)),
+            dma((2,)), dma, dma((3,)), dma,
+            dma((8,)), dma((8,)), dma((8,)), dma((8,)), dma, dma,
         ],
         compiler_params=pltpu.CompilerParams(
             collective_id=0, has_side_effects=True, vmem_limit_bytes=60 << 20

time: 321 us -> 252 us (0.79)
  the two profiles are of different devices: /device:TPU:25 before, /device:TPU:84 now
where the time goes in v3:
time: 252 us; the launch traced here: 251 us
  Pallas kernels  248 us (98%)
  local copies, waits for them, and re-layouts  3.16 us (1%)
    pallas_call x1, Pallas kernels, shards(): pl.pallas_call(kernel, out_shape=jax.ShapeDtypeStruct((PANEL, 1024), F32)...  248 us

profile of v3, /device:TPU:84, one launch (start us, length us, event | category | flops | bytes accessed | tf_op | source)
XLA Modules:
  0.0 251.4 jit_solution(8657429865224817121)
XLA Ops:
  0.0 248.2 %shard_map.46 = f32[512,1024]{1,0:T(8,128)} custom-call(s32[1,16]{1,0:T(1,128)} %t_ref.1, bf16[1,1024,1024]{2,1,0:T(8,128)(2,1)} %v_hbm.1, bf16[1,1024,1024]{2,1,0:T(8,128)(2,1)} %p_hbm.1, bf16[1,1024,1024]{2,1,0:T(8,128)(2,1)} %d_hbm.1), custom_call_target="tpu_custom_call" | custom-call | tf_op jit(solution)/shard_map/pallas_call | solution.py:545
  248.2 3.2 %copy.6 = f32[512,1024]{1,0:T(8,128)} copy(f32[512,1024]{1,0:T(8,128)} %shard_map.46) | data formatting | bytes 4194304

commit v4 on v3

--- a/solution.py
+++ b/solution.py
@@ -12,8 +12,8 @@
 BF16 = jnp.bfloat16
 MESH = pl.DeviceIdType.MESH
 OFFSETS = ((0, 1), (0, 3), (1, 0), (0, 2), (1, 1), (1, 3), (1, 2), (0, 0))
-FIRST_STEPS = 4
-STEPS_PER_BLOCK = 2
+PART = 128
+HALF_ROWS = 2048
 
 
 def tdot(a, b):
@@ -115,10 +115,10 @@
 def kernel(
     t_ref, v_hbm, p_hbm, d_hbm, out_ref,
     rows, V, Pm, Dm, rp, rd, sendq, recvq, ssc, rsc, acc, psc, pqr, pscr,
-    bpart, brecv, bfull, A, inverses, X, work,
+    agq, ags, bpart, brecv, bfull, A, inverses, X, work,
     load_sem, g_recv, g_x, g_z, g_s, pr_send, prs_send, pr_recv, prs_recv, ag_send, ag_recv,
     bq_send, bs_send, bq_recv, bs_recv, c_recv, c_x, c_z, c_s,
-    br_send, br_recv, ba_send, ba_recv, bx_send, bx_recv,
+    br_send, br_recv, ba_send, ba_recv, bx_send, bx_recv, ags_send, ags_recv,
 ):
     c = lax.axis_index("cone")
     b = lax.axis_index("con")
@@ -129,15 +129,19 @@
     sibling = b + 1 - 2 * core
     z_peers = [lax.rem(b + 4 * k, 16) for k in (1, 2, 3)]
 
-    lead = pltpu.make_async_copy(
-        v_hbm.at[0, pl.ds(0, LEAD), :], rows.at[pl.ds(LEAD * b, LEAD), :], load_sem.at[0]
-    )
+    leads = [
+        pltpu.make_async_copy(
+            v_hbm.at[0, pl.ds(PART * h, PART), :],
+            rows.at[pl.ds(HALF_ROWS * h + PART * b, PART), :],
+            load_sem.at[3 + h],
+        )
+        for h in range(2)
+    ]
     loads = [
-        pltpu.make_async_copy(h.at[0], m, load_sem.at[k + 1])
+        pltpu.make_async_copy(h.at[0], m, load_sem.at[k])
         for k, (h, m) in enumerate(((p_hbm, Pm), (d_hbm, Dm), (v_hbm, V)))
     ]
-    lead.start()
-    for load in loads:
+    for load in leads + loads:
         load.start()
 
     barrier = pltpu.get_barrier_semaphore()
@@ -149,61 +153,68 @@
         )
     pl.semaphore_wait(barrier, 12)
 
-    def block_copy(slot, sem, peer):
-        ref = rows.at[pl.ds(pl.multiple_of(LEAD * slot, LEAD), LEAD), :]
+    def block_copy(slot, h, sem, peer):
+        ref = rows.at[pl.ds(pl.multiple_of(HALF_ROWS * h + PART * slot, PART), PART), :]
         return pltpu.make_async_remote_copy(
-            src_ref=ref, dst_ref=ref, send_sem=sem, recv_sem=g_recv.at[slot],
+            src_ref=ref, dst_ref=ref, send_sem=sem, recv_sem=g_recv.at[h, slot],
             device_id={"con": peer}, device_id_type=MESH,
         )
 
-    def to_sibling(slot):
-        return block_copy(slot, g_s.at[slot // 2], sibling)
-
-    def to_z(slot, which):
-        return [block_copy(slot, g_z.at[which, k], z_peers[k]) for k in range(3)]
-
-    lead.wait()
-    to_x = block_copy(b, g_x, x_peer)
-    to_x.start()
-    for copy in to_z(b, 0):
-        copy.start()
-    to_sibling(b).start()
-
-    def arrive(a):
+    def to_x(h):
+        return block_copy(b, h, g_x.at[h], x_peer)
+
+    def to_sibling(slot, h):
+        return block_copy(slot, h, g_s.at[h, slot // 2], sibling)
+
+    def to_z(slot, h, which):
+        return [block_copy(slot, h, g_z.at[h, which, k], z_peers[k]) for k in range(3)]
+
+    def send_on(slot, h, which):
+        for copy in to_z(slot, h, which):
+            copy.start()
+        to_sibling(slot, h).start()
+
+    def take_x(h):
+        block_copy(x_peer, h, g_x.at[h], x_peer).wait_recv()
+        send_on(x_peer, h, 1)
+
+    def arrive(a, h):
         @pl.when(a // 2 != z)
         def _():
             slot = 2 * a + core
-            block_copy(slot, g_x, x_peer).wait_recv()
-            to_sibling(slot).start()
-
-    def arrive_sibling(a):
-        block_copy(2 * a + 1 - core, g_x, x_peer).wait_recv()
+            block_copy(slot, h, g_x.at[h], x_peer).wait_recv()
+            to_sibling(slot, h).start()
+
+    def arrive_sibling(a, h):
+        block_copy(2 * a + 1 - core, h, g_x.at[h], x_peer).wait_recv()
 
     own_flag = t_ref[0, b].astype(F32)
 
     own_chip = b // 2
     contract = (((1,), (1,)), ((), ()))
 
-    def products(a):
-        here = pl.ds(pl.multiple_of(a * PANEL, PANEL), PANEL)
+    def products(a, h, low, high):
+        here = pl.ds(pl.multiple_of(HALF_ROWS * h + LEAD * a, LEAD), LEAD)
 
         @pl.loop(0, 4)
         def _(n):
             cs = pl.ds(pl.multiple_of(n * 256, 256), 256)
-            rp[:, cs] = jnp.dot(rows[here, :], Pm[:, cs], preferred_element_type=F32).astype(BF16)
-            rd[:, cs] = jnp.dot(rows[here, :], Dm[:, cs], preferred_element_type=F32).astype(BF16)
-
-    def grams(a, sink):
+            for matrix, result in ((Pm, rp), (Dm, rd)):
+                value = jnp.dot(rows[here, :], matrix[:, cs], preferred_element_type=F32)
+                result[low : low + PART, cs] = value[:PART].astype(BF16)
+                result[high : high + PART, cs] = value[PART:].astype(BF16)
+
+    def grams(a, count, sink):
         first = t_ref[0, 2 * a].astype(F32) * own_flag
         second = t_ref[0, 2 * a + 1].astype(F32) * own_flag
-        place = lax.broadcasted_iota(jnp.int32, (PANEL, 256), 0)
-        flags = jnp.where(place < LEAD, first, second)
+        place = lax.broadcasted_iota(jnp.int32, (count, 256), 0)
+        flags = jnp.where(place < count // 2, first, second)
 
         @pl.loop(0, 4)
         def _(n):
             cs = pl.ds(pl.multiple_of(n * 256, 256), 256)
-            gp = lax.dot_general(rp[...], V[cs, :], contract, preferred_element_type=F32)
-            gd = lax.dot_general(rd[...], V[cs, :], contract, preferred_element_type=F32)
+            gp = lax.dot_general(rp[:count, :], V[cs, :], contract, preferred_element_type=F32)
+            gd = lax.dot_general(rd[:count, :], V[cs, :], contract, preferred_element_type=F32)
             sink(cs, gp * gd * flags)
 
     def piece(i, size):
@@ -214,7 +225,11 @@
         row_flag = t_ref[0, core].astype(F32)
         place = lax.broadcasted_iota(jnp.int32, (LEAD, PANEL), 1)
         flags = jnp.where(place < LEAD, t_ref[0, 0].astype(F32), t_ref[0, 1].astype(F32)) * row_flag
-        lead_rows = rows[:PANEL, :]
+        lead_rows = jnp.concatenate(
+            [rows[HALF_ROWS * h + PART * k : HALF_ROWS * h + PART * (k + 1), :]
+             for k in range(2) for h in range(2)],
+            axis=0,
+        )
         gp = lax.dot_general(rp[half, :], lead_rows, contract, preferred_element_type=F32)
         gd = lax.dot_general(rd[half, :], lead_rows, contract, preferred_element_type=F32)
         bpart[...] = gp * gd * flags
@@ -263,49 +278,53 @@
         )
 
     def sum_copy(s, slot):
-        ref = X.at[piece(slot, 64), pl.ds(0, 1024)]
-        return pltpu.make_async_remote_copy(
-            src_ref=ref, dst_ref=ref, send_sem=ag_send.at[s], recv_sem=ag_recv.at[slot],
-            device_id={"cone": lax.rem(c + s, 8)}, device_id_type=MESH,
-        )
-
-    def bulk_copy(a, slot):
+        peer = lax.rem(c + s, 8)
         return (
             pltpu.make_async_remote_copy(
-                src_ref=sendq.at[a], dst_ref=recvq.at[slot],
-                send_sem=bq_send.at[a], recv_sem=bq_recv.at[slot],
+                src_ref=agq.at[slot], dst_ref=agq.at[slot],
+                send_sem=ag_send.at[s], recv_sem=ag_recv.at[slot],
+                device_id={"cone": peer}, device_id_type=MESH,
+            ),
+            pltpu.make_async_remote_copy(
+                src_ref=ags.at[slot], dst_ref=ags.at[slot],
+                send_sem=ags_send.at[s], recv_sem=ags_recv.at[slot],
+                device_id={"cone": peer}, device_id_type=MESH,
+            ),
+        )
+
+    def bulk_copy(a, slot, h, part=None):
+        here = piece(h, LEAD) if part is None else piece(2 * h + part, PART)
+        scales = piece(h, 8)
+        return (
+            pltpu.make_async_remote_copy(
+                src_ref=sendq.at[a, here, :], dst_ref=recvq.at[slot, here, :],
+                send_sem=bq_send.at[h, a], recv_sem=bq_recv.at[h, slot],
                 device_id={"cone": a}, device_id_type=MESH,
             ),
             pltpu.make_async_remote_copy(
-                src_ref=ssc.at[a], dst_ref=rsc.at[slot],
-                send_sem=bs_send.at[a], recv_sem=bs_recv.at[slot],
+                src_ref=ssc.at[a, scales, :], dst_ref=rsc.at[slot, scales, :],
+                send_sem=bs_send.at[h, a], recv_sem=bs_recv.at[h, slot],
                 device_id={"cone": a}, device_id_type=MESH,
             ),
         )
 
-    def bulk_part(a, part):
-        here = pl.ds(128 * part, 128)
-        return pltpu.make_async_remote_copy(
-            src_ref=sendq.at[a, here, :], dst_ref=recvq.at[c, here, :],
-            send_sem=bq_send.at[a], recv_sem=bq_recv.at[c],
-            device_id={"cone": a}, device_id_type=MESH,
-        )
-
-    def compute(a):
-        def sink(cs, h):
+    def compute(a, h):
+        here = piece(h, LEAD)
+
+        def sink(cs, value):
             @pl.when(a == c)
             def _():
-                acc[:, cs] = h
+                acc[here, cs] = value
 
             @pl.when(a != c)
             def _():
-                coded, scale = encode(h, 32)
-                sendq[a, :, cs] = coded
-                ssc[a, :, cs] = scale
-
-        arrive_sibling(a)
-        products(a)
-        grams(a, sink)
+                coded, scale = encode(value, 32)
+                sendq[a, here, cs] = coded
+                ssc[a, piece(h, 8), cs] = scale
+
+        arrive_sibling(a, h)
+        products(a, h, 0, PART)
+        grams(a, LEAD, sink)
 
     def target(t):
         dx = dy = 0
@@ -314,41 +333,52 @@
             dy = jnp.where(t == k + 1, y, dy)
         return lax.rem(c // 4 + dx, 2) * 4 + lax.rem(lax.rem(c, 4) + dy, 4)
 
-    def issue(low, high):
-        for part in range(4):
+    def issue(low, high, h):
+        for part in range(2):
             for t in range(low, high):
                 a = target(t)
 
                 @pl.when(a != 0)
                 def _():
+                    coded, scale = bulk_copy(a, c, h, part)
                     if part == 0:
-                        bulk_copy(a, c)[1].start()
-                    bulk_part(a, part).start()
-
-    def bulk_step(t):
-        a = target(t)
-        follow = target(t + 1)
-
-        @pl.when((t < 8) & (follow != 0))
-        def _():
-            arrive(follow)
-
-        @pl.when((a != 0) & (a != own_chip))
-        def _():
-            compute(a)
-
-        @pl.when((t == 3))
-        def _():
-            issue(1, 4)
-
-        @pl.when((t == 7))
-        def _():
-            issue(4, 8)
-
-    def bulk(low, high):
+                        scale.start()
+                    coded.start()
+
+    def bulk(low, high, h):
         @pl.loop(low, high)
         def _(t):
-            bulk_step(t)
+            a = target(t)
+
+            @pl.when(a != 0)
+            def _():
+                compute(a, h)
+
+            @pl.when(t == 3)
+            def _():
+                issue(1, 4, h)
+
+            @pl.when(t == 7)
+            def _():
+                issue(4, 8, h)
+
+    def arrive_all(h):
+        @pl.loop(1, 8)
+        def _(a):
+            arrive(a, h)
+
+    def accumulate(h):
+        @pl.loop(1, 8)
+        def _(s):
+            source = lax.rem(c + s, 8)
+            for copy in bulk_copy(source, source, h):
+                copy.wait_recv()
+            for r in range(2):
+                part = piece(2 * h + r, PART)
+                scales = rsc[source, piece(h, 8), :]
+                acc[part, :] = acc[part, :] + decode(
+                    recvq[source, part, :], scales[4 * r : 4 * r + 4], 32
+                )
 
     def spread_copy(slot, sem, peer):
         ref = X.at[:, pl.ds(pl.multiple_of(1024 + slot * LEAD, LEAD), LEAD)]
@@ -396,26 +426,43 @@
         def _():
             spread_copy(core, c_x, x_peer).wait_send()
 
+    for lead in leads:
+        lead.wait()
+    for h in range(2):
+        to_x(h).start()
+    send_on(b, 0, 0)
+
+    @pl.when(own_chip == 0)
+    def _():
+        send_on(b, 1, 0)
+
     for load in loads:
         load.wait()
-
-    @pl.when(own_chip != 0)
+    take_x(0)
+
+    @pl.when(x_peer // 2 == 0)
     def _():
-        compute(own_chip)
-
-    block_copy(x_peer, g_x, x_peer).wait_recv()
-    for copy in to_z(x_peer, 1):
-        copy.start()
-    to_sibling(x_peer).start()
-
-    arrive(0)
-    arrive_sibling(0)
-    products(0)
+        take_x(1)
+
+    for h in range(2):
+        arrive(0, h)
+    for h in range(2):
+        arrive_sibling(0, h)
+        products(0, h, PART * h, LEAD + PART * h)
     pivot_part()
     for s in range(1, 8):
         pivot_copy(s, c).start()
 
-    grams(0, panel_sink)
+    grams(0, PANEL, panel_sink)
+    arrive_all(0)
+
+    @pl.when(own_chip != 0)
+    def _():
+        send_on(b, 1, 0)
+
+    @pl.when(x_peer // 2 != 0)
+    def _():
+        take_x(1)
 
     half_piece = piece(c, 32)
     bfull[core, half_piece, :] = bpart[half_piece, :]
@@ -432,13 +479,7 @@
         for copy in panel_copy(s, c):
             copy.start()
 
-    follow = target(1)
-
-    @pl.when(follow != 0)
-    def _():
-        arrive(follow)
-
-    bulk(1, FIRST_STEPS)
+    bulk(1, 4, 0)
 
     for s in range(1, 8):
         pivot_sum_copy(s, lax.rem(c + s, 8)).wait_recv()
@@ -453,8 +494,13 @@
             copy.wait_recv()
         X[mine, :1024] = X[mine, :1024] + decode(pqr[source], pscr[source], 8)
 
+    agq[c], ags[c] = encode(X[mine, :1024], 8)
     for s in range(1, 8):
-        sum_copy(s, c).start()
+        for copy in sum_copy(s, c):
+            copy.start()
+
+    bulk(4, 9, 0)
+    arrive_all(1)
 
     pivot_half_copy(1 - core).wait_recv()
     A[:LEAD, :] = bfull[0]
@@ -463,12 +509,21 @@
 
     @pl.loop(0, 4)
     def _(k):
+        low = jnp.where(k == 0, 1, jnp.where(k == 1, 4, 9))
+        high = jnp.where(k == 0, 4, 9)
+        bulk(low, high, 1)
         factor_step(k, A, inverses, work)
 
         @pl.when(k == 1)
         def _():
             for s in range(1, 8):
-                sum_copy(s, lax.rem(c + s, 8)).wait_recv()
+                for copy in sum_copy(s, lax.rem(c + s, 8)):
+                    copy.wait_recv()
+
+            @pl.loop(0, 8)
+            def _(s):
+                X[piece(s, 64), :1024] = decode(agq[s], ags[s], 8)
+
             spread_start()
 
         @pl.when(k == 2)
@@ -479,58 +534,50 @@
         def _():
             spread_relay_far()
 
-        low = FIRST_STEPS + STEPS_PER_BLOCK * k
-        bulk(low, jnp.where(k == 3, 9, jnp.minimum(low + STEPS_PER_BLOCK, 9)))
+    @pl.when(c != 0)
+    def _():
+        accumulate(0)
 
     spread_copy(1 - core, c_s, sibling).wait_recv()
     spread_end()
-    for s in range(1, 8):
-        sum_copy(s, c).wait_send()
     substitute(A, inverses, X)
 
     @pl.when(c != 0)
     def _():
-        @pl.loop(1, 8)
-        def _(s):
-            source = lax.rem(c + s, 8)
-            for copy in bulk_copy(source, source):
-                copy.wait_recv()
-            for r in range(4):
-                part = pl.ds(r * 128, 128)
-                acc[part, :] = acc[part, :] + decode(
-                    recvq[source, part, :], rsc[source, pl.ds(r * 4, 4), :], 32
-                )
+        accumulate(1)
 
         @pl.loop(0, 4)
-        def _(r):
-            part = block(r)
+        def _(q):
+            r = 2 * (q % 2) + q // 2
             change = tdot(X[:, block(8 + r)], X[:, :1024])
             place = lax.broadcasted_iota(jnp.int32, (128, 1024), 1)
             gone = (place < LEAD) & (b < 2)
-            out_ref[part, :] = jnp.where(gone, 0.0, acc[part, :] - change)
+            out_ref[block(r), :] = jnp.where(gone, 0.0, acc[block(q), :] - change)
 
     @pl.when(c == 0)
     def _():
         out_ref[...] = X[:, :1024]
 
-    to_x.wait_send()
-    for copy in to_z(b, 0) + to_z(x_peer, 1):
-        copy.wait_send()
-
-    @pl.loop(0, 8)
-    def _(a):
-        to_sibling(2 * a + core).wait_send()
+    for h in range(2):
+        to_x(h).wait_send()
+        for copy in to_z(b, h, 0) + to_z(x_peer, h, 1):
+            copy.wait_send()
+
+        @pl.loop(0, 8)
+        def _(a):
+            to_sibling(2 * a + core, h).wait_send()
 
     for s in range(1, 8):
-        for copy in panel_copy(s, c):
+        for copy in panel_copy(s, c) + sum_copy(s, c):
             copy.wait_send()
 
         a = lax.rem(c + s, 8)
 
         @pl.when(a != 0)
         def _():
-            for copy in bulk_copy(a, c):
-                copy.wait_send()
+            for h in range(2):
+                for copy in bulk_copy(a, c, h):
+                    copy.wait_send()
 
         pivot_copy(s, c).wait_send()
         pivot_sum_copy(s, c).wait_send()
@@ -562,6 +609,8 @@
             vmem((64, 1024), F32),
             vmem((8, 64, 1024), jnp.int16),
             vmem((8, 8, 1024), F32),
+            vmem((8, 64, 1024), jnp.int16),
+            vmem((8, 8, 1024), F32),
             vmem((LEAD, PANEL), F32),
             vmem((8, 32, PANEL), F32),
             vmem((2, LEAD, PANEL), F32),
@@ -569,11 +618,11 @@
             vmem((4, 128, 128), F32),
             vmem((PANEL, 1536), F32),
             vmem((128, 256), F32),
-            dma((4,)), dma((16,)), dma, dma((2, 3)), dma((8,)),
+            dma((5,)), dma((2, 16)), dma((2,)), dma((2, 2, 3)), dma((2, 8)),
             dma((8,)), dma((8,)), dma((8,)), dma((8,)), dma((8,)), dma((8,)),
-            dma((8,)), dma((8,)), dma((8,)), dma((8,)),
+            dma((2, 8)), dma((2, 8)), dma((2, 8)), dma((2, 8)),
             dma((2,)), dma, dma((3,)), dma,
-            dma((8,)), dma((8,)), dma((8,)), dma((8,)), dma, dma,
+            dma((8,)), dma((8,)), dma((8,)), dma((8,)), dma, dma, dma((8,)), dma((8,)),
         ],
         compiler_params=pltpu.CompilerParams(
             collective_id=0, has_side_effects=True, vmem_limit_bytes=60 << 20

time: 252 us -> 238 us (0.944)
  the two profiles are of different devices: /device:TPU:84 before, /device:TPU:25 now
where the time goes in v4:
time: 238 us
  Pallas kernels  235 us (99%)
  local copies, waits for them, and re-layouts  3.16 us (1%)
    pallas_call x1, Pallas kernels, shards(): pl.pallas_call(kernel, out_shape=jax.ShapeDtypeStruct((PANEL, 1024), F32)...  235 us

profile of v4, /device:TPU:25, one launch (start us, length us, event | category | flops | bytes accessed | tf_op | source)
XLA Modules:
  0.0 238.2 jit_solution(9923518663171443612)
XLA Ops:
  0.0 235.0 %shard_map.46 = f32[512,1024]{1,0:T(8,128)} custom-call(s32[1,16]{1,0:T(1,128)} %t_ref.1, bf16[1,1024,1024]{2,1,0:T(8,128)(2,1)} %v_hbm.1, bf16[1,1024,1024]{2,1,0:T(8,128)(2,1)} %p_hbm.1, bf16[1,1024,1024]{2,1,0:T(8,128)(2,1)} %d_hbm.1), custom_call_target="tpu_custom_call" | custom-call | tf_op jit(solution)/shard_map/pallas_call | solution.py:592
  235.0 3.2 %copy.6 = f32[512,1024]{1,0:T(8,128)} copy(f32[512,1024]{1,0:T(8,128)} %shard_map.46) | data formatting | bytes 4194304

commit v5 on v4

--- a/solution.py
+++ b/solution.py
@@ -115,9 +115,9 @@
 def kernel(
     t_ref, v_hbm, p_hbm, d_hbm, out_ref,
     rows, V, Pm, Dm, rp, rd, sendq, recvq, ssc, rsc, acc, psc, pqr, pscr,
-    agq, ags, bpart, brecv, bfull, A, inverses, X, work,
+    agq, ags, spq, sps, bpart, brecv, bfull, A, inverses, X, work,
     load_sem, g_recv, g_x, g_z, g_s, pr_send, prs_send, pr_recv, prs_recv, ag_send, ag_recv,
-    bq_send, bs_send, bq_recv, bs_recv, c_recv, c_x, c_z, c_s,
+    bq_send, bs_send, bq_recv, bs_recv, c_recv, c_send,
     br_send, br_recv, ba_send, ba_recv, bx_send, bx_recv, ags_send, ags_recv,
 ):
     c = lax.axis_index("cone")
@@ -354,9 +354,10 @@
             def _():
                 compute(a, h)
 
-            @pl.when(t == 3)
-            def _():
-                issue(1, 4, h)
+            if h == 1:
+                @pl.when(t == 3)
+                def _():
+                    issue(1, 4, h)
 
             @pl.when(t == 7)
             def _():
@@ -380,51 +381,66 @@
                     recvq[source, part, :], scales[4 * r : 4 * r + 4], 32
                 )
 
-    def spread_copy(slot, sem, peer):
-        ref = X.at[:, pl.ds(pl.multiple_of(1024 + slot * LEAD, LEAD), LEAD)]
-        return pltpu.make_async_remote_copy(
-            src_ref=ref, dst_ref=ref, send_sem=sem, recv_sem=c_recv.at[slot],
-            device_id={"con": peer}, device_id_type=MESH,
-        )
+    def spread_copy(slot, place, peer):
+        return [
+            pltpu.make_async_remote_copy(
+                src_ref=ref.at[slot], dst_ref=ref.at[slot],
+                send_sem=c_send.at[kind, place], recv_sem=c_recv.at[kind, slot],
+                device_id={"con": peer}, device_id_type=MESH,
+            )
+            for kind, ref in enumerate((spq, sps))
+        ]
 
     at_home_z = z == c // 2
     at_home_x = xh == lax.rem(c, 2)
 
+    def spread_take(slot):
+        for copy in spread_copy(slot, 0, sibling):
+            copy.wait_recv()
+
+    def spread_send(place, peer, sent=False):
+        for copy in spread_copy(core, place, peer):
+            if sent:
+                copy.wait_send()
+            else:
+                copy.start()
+
     def spread_on():
         for k in range(3):
-            spread_copy(core, c_z.at[k], z_peers[k]).start()
-        spread_copy(core, c_s, sibling).start()
+            spread_send(2 + k, z_peers[k])
+        spread_send(0, sibling)
 
     def spread_start():
         @pl.when(at_home_z & at_home_x)
         def _():
-            X[:, pl.ds(pl.multiple_of(1024 + core * LEAD, LEAD), LEAD)] = X[:, :LEAD]
-            spread_copy(core, c_x, x_peer).start()
+            spq[core] = agq[:, :, :LEAD]
+            sps[core] = ags[:, :, :LEAD]
+            spread_send(1, x_peer)
             spread_on()
 
     def spread_relay():
         @pl.when(at_home_z & (xh != lax.rem(c, 2)))
         def _():
-            spread_copy(core, c_x, x_peer).wait_recv()
+            spread_take(core)
             spread_on()
 
     def spread_relay_far():
         @pl.when(z != c // 2)
         def _():
-            spread_copy(core, c_x, x_peer).wait_recv()
-            spread_copy(core, c_s, sibling).start()
+            spread_take(core)
+            spread_send(0, sibling)
 
     def spread_end():
-        spread_copy(core, c_s, sibling).wait_send()
+        spread_send(0, sibling, sent=True)
 
         @pl.when(at_home_z)
         def _():
             for k in range(3):
-                spread_copy(core, c_z.at[k], z_peers[k]).wait_send()
+                spread_send(2 + k, z_peers[k], sent=True)
 
         @pl.when(at_home_z & at_home_x)
         def _():
-            spread_copy(core, c_x, x_peer).wait_send()
+            spread_send(1, x_peer, sent=True)
 
     for lead in leads:
         lead.wait()
@@ -499,8 +515,18 @@
         for copy in sum_copy(s, c):
             copy.start()
 
+    issue(1, 4, 0)
     bulk(4, 9, 0)
     arrive_all(1)
+
+    for s in range(1, 8):
+        for copy in sum_copy(s, lax.rem(c + s, 8)):
+            copy.wait_recv()
+    spread_start()
+
+    @pl.loop(0, 8)
+    def _(s):
+        X[piece(s, 64), :1024] = decode(agq[s], ags[s], 8)
 
     pivot_half_copy(1 - core).wait_recv()
     A[:LEAD, :] = bfull[0]
@@ -514,23 +540,11 @@
         bulk(low, high, 1)
         factor_step(k, A, inverses, work)
 
+        @pl.when(k == 0)
+        def _():
+            spread_relay()
+
         @pl.when(k == 1)
-        def _():
-            for s in range(1, 8):
-                for copy in sum_copy(s, lax.rem(c + s, 8)):
-                    copy.wait_recv()
-
-            @pl.loop(0, 8)
-            def _(s):
-                X[piece(s, 64), :1024] = decode(agq[s], ags[s], 8)
-
-            spread_start()
-
-        @pl.when(k == 2)
-        def _():
-            spread_relay()
-
-        @pl.when(k == 3)
         def _():
             spread_relay_far()
 
@@ -538,8 +552,14 @@
     def _():
         accumulate(0)
 
-    spread_copy(1 - core, c_s, sibling).wait_recv()
-    spread_end()
+    spread_take(1 - core)
+
+    @pl.loop(0, 8)
+    def _(s):
+        for slot in range(2):
+            low = 1024 + slot * LEAD
+            X[piece(s, 64), low : low + LEAD] = decode(spq[slot, s], sps[slot, s], 8)
+
     substitute(A, inverses, X)
 
     @pl.when(c != 0)
@@ -583,6 +603,7 @@
         pivot_sum_copy(s, c).wait_send()
 
     pivot_half_copy(core).wait_send()
+    spread_end()
 
 
 def shards(vectors, primal, dual_inverse, touches):
@@ -611,6 +632,8 @@
             vmem((8, 8, 1024), F32),
             vmem((8, 64, 1024), jnp.int16),
             vmem((8, 8, 1024), F32),
+            vmem((2, 8, 64, LEAD), jnp.int16),
+            vmem((2, 8, 8, LEAD), F32),
             vmem((LEAD, PANEL), F32),
             vmem((8, 32, PANEL), F32),
             vmem((2, LEAD, PANEL), F32),
@@ -621,7 +644,7 @@
             dma((5,)), dma((2, 16)), dma((2,)), dma((2, 2, 3)), dma((2, 8)),
             dma((8,)), dma((8,)), dma((8,)), dma((8,)), dma((8,)), dma((8,)),
             dma((2, 8)), dma((2, 8)), dma((2, 8)), dma((2, 8)),
-            dma((2,)), dma, dma((3,)), dma,
+            dma((2, 2)), dma((2, 5)),
             dma((8,)), dma((8,)), dma((8,)), dma((8,)), dma, dma, dma((8,)), dma((8,)),
         ],
         compiler_params=pltpu.CompilerParams(

time: 238 us -> 219 us (0.920)
  the two profiles are of different devices: /device:TPU:25 before, /device:TPU:56 now
where the time goes in v5:
time: 219 us
  Pallas kernels  216 us (99%)
  local copies, waits for them, and re-layouts  3.16 us (1%)
    pallas_call x1, Pallas kernels, shards(): pl.pallas_call(kernel, out_shape=jax.ShapeDtypeStruct((PANEL, 1024), F32)...  216 us

profile of v5, /device:TPU:56, one launch (start us, length us, event | category | flops | bytes accessed | tf_op | source)
XLA Modules:
  0.0 218.8 jit_solution(16637301681050003755)
XLA Ops:
  0.0 215.6 %shard_map.46 = f32[512,1024]{1,0:T(8,128)} custom-call(s32[1,16]{1,0:T(1,128)} %t_ref.1, bf16[1,1024,1024]{2,1,0:T(8,128)(2,1)} %v_hbm.1, bf16[1,1024,1024]{2,1,0:T(8,128)(2,1)} %p_hbm.1, bf16[1,1024,1024]{2,1,0:T(8,128)(2,1)} %d_hbm.1), custom_call_target="tpu_custom_call" | custom-call | tf_op jit(solution)/shard_map/pallas_call | solution.py:613
  215.6 3.2 %copy.6 = f32[512,1024]{1,0:T(8,128)} copy(f32[512,1024]{1,0:T(8,128)} %shard_map.46) | data formatting | bytes 4194304

commit v6 on v5

--- a/solution.py
+++ b/solution.py
@@ -359,9 +359,10 @@
                 def _():
                     issue(1, 4, h)
 
-            @pl.when(t == 7)
-            def _():
-                issue(4, 8, h)
+            if h == 1:
+                @pl.when(t == 7)
+                def _():
+                    issue(4, 8, h)
 
     def arrive_all(h):
         @pl.loop(1, 8)
@@ -523,6 +524,7 @@
         for copy in sum_copy(s, lax.rem(c + s, 8)):
             copy.wait_recv()
     spread_start()
+    issue(4, 8, 0)
 
     @pl.loop(0, 8)
     def _(s):

time: 219 us -> 212 us (0.968)
  the two profiles are of different devices: /device:TPU:56 before, /device:TPU:86 now
where the time goes in v6:
time: 212 us
  Pallas kernels  209 us (99%)
  local copies, waits for them, and re-layouts  3.16 us (1%)
    pallas_call x1, Pallas kernels, shards(): pl.pallas_call(kernel, out_shape=jax.ShapeDtypeStruct((PANEL, 1024), F32)...  209 us

profile of v6, /device:TPU:86, one launch (start us, length us, event | category | flops | bytes accessed | tf_op | source)
XLA Modules:
  0.0 212.1 jit_solution(13556322801864408111)
XLA Ops:
  0.0 208.9 %shard_map.46 = f32[512,1024]{1,0:T(8,128)} custom-call(s32[1,16]{1,0:T(1,128)} %t_ref.1, bf16[1,1024,1024]{2,1,0:T(8,128)(2,1)} %v_hbm.1, bf16[1,1024,1024]{2,1,0:T(8,128)(2,1)} %p_hbm.1, bf16[1,1024,1024]{2,1,0:T(8,128)(2,1)} %d_hbm.1), custom_call_target="tpu_custom_call" | custom-call | tf_op jit(solution)/shard_map/pallas_call | solution.py:615
  208.9 3.2 %copy.6 = f32[512,1024]{1,0:T(8,128)} copy(f32[512,1024]{1,0:T(8,128)} %shard_map.46) | data formatting | bytes 4194304

commit v7 on v6

--- a/solution.py
+++ b/solution.py
@@ -516,7 +516,6 @@
         for copy in sum_copy(s, c):
             copy.start()
 
-    issue(1, 4, 0)
     bulk(4, 9, 0)
     arrive_all(1)
 
@@ -524,7 +523,7 @@
         for copy in sum_copy(s, lax.rem(c + s, 8)):
             copy.wait_recv()
     spread_start()
-    issue(4, 8, 0)
+    issue(1, 8, 0)
 
     @pl.loop(0, 8)
     def _(s):

time: 212 us -> 216 us (1.019)
  the two profiles are of different devices: /device:TPU:86 before, /device:TPU:38 now
where the time goes in v7:
time: 216 us
  Pallas kernels  213 us (99%)
  local copies, waits for them, and re-layouts  3.16 us (1%)
    pallas_call x1, Pallas kernels, shards(): pl.pallas_call(kernel, out_shape=jax.ShapeDtypeStruct((PANEL, 1024), F32)...  213 us

profile of v7, /device:TPU:38, one launch (start us, length us, event | category | flops | bytes accessed | tf_op | source)
XLA Modules:
  0.0 216.1 jit_solution(2410994649431198718)
XLA Ops:
  0.0 212.9 %shard_map.46 = f32[512,1024]{1,0:T(8,128)} custom-call(s32[1,16]{1,0:T(1,128)} %t_ref.1, bf16[1,1024,1024]{2,1,0:T(8,128)(2,1)} %v_hbm.1, bf16[1,1024,1024]{2,1,0:T(8,128)(2,1)} %p_hbm.1, bf16[1,1024,1024]{2,1,0:T(8,128)(2,1)} %d_hbm.1), custom_call_target="tpu_custom_call" | custom-call | tf_op jit(solution)/shard_map/pallas_call | solution.py:614
  212.9 3.2 %copy.6 = f32[512,1024]{1,0:T(8,128)} copy(f32[512,1024]{1,0:T(8,128)} %shard_map.46) | data formatting | bytes 4194304

commit v8 on v6

--- a/solution.py
+++ b/solution.py
@@ -471,6 +471,9 @@
         pivot_copy(s, c).start()
 
     grams(0, PANEL, panel_sink)
+    for s in range(1, 8):
+        for copy in panel_copy(s, c):
+            copy.start()
     arrive_all(0)
 
     @pl.when(own_chip != 0)
@@ -492,9 +495,6 @@
 
     for s in range(1, 8):
         pivot_sum_copy(s, c).start()
-    for s in range(1, 8):
-        for copy in panel_copy(s, c):
-            copy.start()
 
     bulk(1, 4, 0)
 

time: 212 us -> 212 us (level)
  the two profiles are of different devices: /device:TPU:86 before, /device:TPU:38 now
where the time goes in v8:
time: 212 us
  Pallas kernels  209 us (99%)
  local copies, waits for them, and re-layouts  3.16 us (1%)
    pallas_call x1, Pallas kernels, shards(): pl.pallas_call(kernel, out_shape=jax.ShapeDtypeStruct((PANEL, 1024), F32)...  209 us

profile of v8, /device:TPU:38, one launch (start us, length us, event | category | flops | bytes accessed | tf_op | source)
XLA Modules:
  0.0 211.9 jit_solution(11078536869950698631)
XLA Ops:
  0.0 208.7 %shard_map.46 = f32[512,1024]{1,0:T(8,128)} custom-call(s32[1,16]{1,0:T(1,128)} %t_ref.1, bf16[1,1024,1024]{2,1,0:T(8,128)(2,1)} %v_hbm.1, bf16[1,1024,1024]{2,1,0:T(8,128)(2,1)} %p_hbm.1, bf16[1,1024,1024]{2,1,0:T(8,128)(2,1)} %d_hbm.1), custom_call_target="tpu_custom_call" | custom-call | tf_op jit(solution)/shard_map/pallas_call | solution.py:615
  208.7 3.2 %copy.6 = f32[512,1024]{1,0:T(8,128)} copy(f32[512,1024]{1,0:T(8,128)} %shard_map.46) | data formatting | bytes 4194304
